TPU v7x, 512 devices: a whole 4x4x16 slice. The times are simulated.
512 devices in a mesh: section: 2 (over x_lo), chan: 128 (over y, z, core), win: 2 (over x_hi).
Axes of the slice: x: 4 (x_hi: 2, x_lo: 2; x = x_hi * 2 + x_lo), y: 4, z: 16, core: 2. Of those that a mesh axis runs over, the one named last changes fastest.
Arguments:
- raw: bfloat16 [8, 1024, 640], P(('section', 'win'), 'chan'), may hold values from -6 to 6
- flags: int32 [8, 1024], P(('section', 'win'), 'chan'), may hold values from 0 to 1, as said below
- in_weight: bfloat16 [32, 3], replicated, may hold values from -3.5 to 3.5
- conv_weight: bfloat16 [3, 32, 32, 3, 3], replicated, may hold values from -0.375 to 0.375
- out_weight: bfloat16 [32], replicated, may hold values from -1 to 1
- sources: int32 [128], replicated, may hold values from 0 to 1023
Outputs:
- coherency: float32 [256, 2, 128, 1024], P(('section', 'chan'), None, None, 'win')
Inputs may be any that keep to these rules, and one draw needn't show every extreme that they name: `flags`: some channels have no valid window at all, and some exactly one.
All inputs are finite; a program needn't handle non-finite values.
Results may differ from a plain program's by a relative error of at most 0.04.
Values may be sent and summed in bfloat16 or wider, within the bound.
No kernel may reach another device: no remote copies, remote signals or barrier semaphores. Data moves between devices by JAX's collectives and lax.ppermute only.
A program may use at most 64 MiB of HBM per device.

v0:
```python
import functools
import math

import jax
import jax.numpy as jnp
import numpy as np
from jax import lax
from jax.experimental import pallas as pl
from jax.experimental.pallas import tpu as pltpu
from jax.sharding import Mesh, PartitionSpec as P

NT = 640
F = 32
LAYERS = 3
NF = 256
OWN = 8
WIN = 2
EXT = OWN + 2 * LAYERS
BLK = 6
WIDE = WIN * NT

water_level = 0.2
epsilon_power = 1e-06

F32 = jnp.float32
BF16 = jnp.bfloat16


def dft_table():
    part, z, core, y, section = np.meshgrid(
        np.arange(2), np.arange(16), np.arange(2), np.arange(4), np.arange(2), indexing="ij"
    )
    k = (section * 128 + (y * 16 + z) * 2 + core).reshape(-1)
    part = part.reshape(-1)
    phases = np.arange(NT)[:, None] * (k + 1)[None, :] % NT
    angles = phases.astype(np.float32) * np.float32(2.0 * math.pi / NT)
    table = np.where(part[None, :] == 0, np.cos(angles), -np.sin(angles))
    return table.astype(BF16)


def iota(shape, dim):
    return lax.broadcasted_iota(jnp.int32, shape, dim)


def column(row, n):
    eye = iota((n, n), 0) == iota((n, n), 1)
    return jnp.sum(jnp.where(eye, jnp.broadcast_to(row, (n, n)), 0.0), axis=1, keepdims=True)


def swap_bits(x, row_step, lane_step):
    rows, lanes = x.shape
    row_bit = (iota(x.shape, 0) // row_step) % 2
    lane_bit = (iota(x.shape, 1) // lane_step) % 2
    down = pltpu.roll(pltpu.roll(x, rows - row_step, 0), lane_step, 1)
    up = pltpu.roll(pltpu.roll(x, row_step, 0), lanes - lane_step, 1)
    return jnp.where(row_bit == lane_bit, x, jnp.where(row_bit == 0, down, up))


def prepare_kernel(conv_ref, in_ref, out_ref, band_ref, first_ref, last_ref):
    for layer in range(LAYERS):
        for tap in range(3):
            taps = [conv_ref[layer, a, tap].astype(F32) for a in range(3)]
            base = jnp.concatenate(taps + [jnp.zeros((F, 256 - 3 * F), F32)], axis=1)
            for c in range(BLK):
                row = base if c == 0 else pltpu.roll(base, F * c, 1)
                band_ref[layer, tap, F * c : F * (c + 1), :] = row.astype(BF16)
    shape = (EXT * F, 72)
    channel = iota(shape, 0) // F
    place = jnp.where(channel < 3, 13 + channel, jnp.where(channel < 11, channel - 3, channel + 5))
    lane = iota(shape, 1)
    first = jnp.zeros(shape, F32)
    for tap in range(3):
        weight = column(in_ref[tap : tap + 1, :].astype(F32), F)
        tall = jnp.broadcast_to(jnp.concatenate([weight] * EXT, axis=0), shape)
        first = jnp.where(lane == place + 24 * tap, tall, first)
    first_ref[...] = first.astype(BF16)
    shape = (OWN, OWN * F)
    wide = jnp.concatenate([out_ref[...].astype(F32)] * OWN, axis=1)
    last_ref[...] = jnp.where(
        iota(shape, 0) == iota(shape, 1) // F, jnp.broadcast_to(wide, shape), 0.0
    ).astype(BF16)


def shifted(x, step):
    time = iota(x.shape, 1) % NT
    moved = pltpu.roll(x, step % WIDE, 1)
    keep = (time >= step) if step > 0 else (time < NT + step)
    return jnp.where(keep, moved, jnp.zeros_like(moved))


def denoise_kernel(
    edge_ref, left_ref, raw_ref, right_ref, flags_ref, band_ref, first_ref, last_ref, table_ref,
    out_ref, taps_ref, next_ref, line_ref,
):
    is_first, is_last = edge_ref[0], edge_ref[1]
    rows = jnp.concatenate(
        [
            jnp.concatenate([ref[w].astype(F32) for w in range(WIN)], axis=1)
            for ref in (raw_ref, left_ref, right_ref)
        ],
        axis=0,
    )
    lines = jnp.concatenate([shifted(rows, 1), rows, shifted(rows, -1)], axis=0).astype(BF16)
    for n in range(0, WIDE, 256):
        next_ref[:, n : n + 256] = jnp.dot(
            first_ref[...], lines[:, n : n + 256], preferred_element_type=F32
        ).astype(BF16)
    count = EXT
    for layer in range(LAYERS):
        step = 2**layer
        for r in range(0, count * F, F):
            block = next_ref[r : r + F, :].astype(F32)
            taps_ref[0, r : r + F, :] = shifted(block, step).astype(BF16)
            taps_ref[1, r : r + F, :] = next_ref[r : r + F, :]
            taps_ref[2, r : r + F, :] = shifted(block, -step).astype(BF16)
        count -= 2
        for c in range(0, count, BLK):
            size = min(BLK, count - c)
            for n in range(0, WIDE, 256):
                total = None
                for tap in range(3):
                    term = jnp.dot(
                        band_ref[layer, tap, : size * F, : (size + 2) * F],
                        taps_ref[tap, c * F : (c + size + 2) * F, n : n + 256],
                        preferred_element_type=F32,
                    )
                    total = term if total is None else total + term
                old = taps_ref[1, (c + 1) * F : (c + 1 + size) * F, n : n + 256].astype(F32)
                new = old + jnp.maximum(total, 0.0)
                reach = LAYERS - 1 - layer
                for k in range(size):
                    part = new[k * F : (k + 1) * F]
                    if c + k < reach:
                        part = jnp.where(is_first == 1, 0.0, part)
                    if c + k >= count - reach:
                        part = jnp.where(is_last == 1, 0.0, part)
                    next_ref[(c + k) * F : (c + k + 1) * F, n : n + 256] = part.astype(BF16)
    clean = jnp.dot(last_ref[...], next_ref[: OWN * F, :], preferred_element_type=F32)
    clean = jnp.concatenate([clean[:, w * NT : (w + 1) * NT] for w in range(WIN)], axis=0)
    spectra = jnp.dot(clean.astype(BF16), table_ref[...], preferred_element_type=F32)
    real, imag = spectra[:, :NF], spectra[:, NF:]
    power = real * real + imag * imag
    spread = jnp.sqrt(jnp.mean(power, axis=1, keepdims=True) + epsilon_power)
    flags = jnp.concatenate(
        [column(flags_ref[w : w + 1, :].astype(F32), OWN) for w in range(WIN)], axis=0
    )
    factor = flags / (jnp.sqrt(power) + water_level * spread)
    for part, value in enumerate((real * factor, imag * factor)):
        for w in range(WIN):
            for high in range(2):
                x = value[w * OWN : (w + 1) * OWN, high * 128 : (high + 1) * 128]
                for bit in range(3):
                    x = swap_bits(x, 2**bit, 16 * 2**bit)
                line_ref[pl.ds(32 * high + 2 * w + part, 8, stride=4), :] = x
    out_ref[...] = line_ref[...].astype(BF16)


def turn_kernel(in_ref, out_ref):
    x = in_ref[...].astype(F32)
    for bit in range(4):
        x = swap_bits(x, 4 * 2**bit, 2**bit)
    x = x.astype(BF16)
    out_ref[:64, :] = x
    out_ref[64:, :] = x


def coherence_kernel(half_ref, sources_ref, in_ref, out_ref, all_ref):
    x = in_ref[...].astype(F32)

    def piece(w, c, y):
        start = ((w * 2 + c) * 4 + y) * 8
        return x[start : start + 8]

    stacked = jnp.concatenate(
        [
            jnp.concatenate([piece(w, c, y) for y in range(4) for w in range(2)], axis=0)
            for c in range(2)
        ],
        axis=1,
    ).astype(BF16)
    shape = (256, 256)
    r = iota(shape, 0)
    target = (r % 16) * 16 + (r // 128) * 8 + (r // 16) % 8
    perm = jnp.where(target == iota(shape, 1), 1.0, 0.0).astype(BF16)
    ordered = jnp.dot(stacked, perm, preferred_element_type=F32)
    every = jnp.concatenate([ordered[16 * y : 16 * (y + 1)] for y in range(4)], axis=1)
    all_ref[...] = every
    half = half_ref[0]
    receivers = all_ref[:, pl.ds(pl.multiple_of(half * 512, 512), 512)]
    shape = (CH_ALL, 128)
    one_hot = jnp.where(
        iota(shape, 0) == jnp.broadcast_to(sources_ref[...], shape), 1.0, 0.0
    ).astype(BF16)
    chosen = jnp.dot(every.astype(BF16), one_hot, preferred_element_type=F32)
    even = iota(receivers.shape, 0) % 2 == 0
    turned = jnp.where(even, pltpu.roll(receivers, 15, 0), -pltpu.roll(receivers, 1, 0))
    chosen_t = chosen.T
    energy_src = jnp.sum(chosen_t * chosen_t, axis=1, keepdims=True)
    energy_rec = jnp.sum(receivers * receivers, axis=0, keepdims=True)
    scale = lax.rsqrt(jnp.maximum(energy_src * energy_rec, 1.0))
    left = chosen_t.astype(BF16)
    out_ref[0, 0] = jnp.dot(left, receivers.astype(BF16), preferred_element_type=F32) * scale
    out_ref[0, 1] = jnp.dot(left, turned.astype(BF16), preferred_element_type=F32) * scale


CH_ALL = 1024

VMEM = pl.BlockSpec(memory_space=pltpu.VMEM)
SMEM = pl.BlockSpec(memory_space=pltpu.SMEM)
PARAMS = pltpu.CompilerParams(vmem_limit_bytes=32 * 1024 * 1024)


def prepare(conv_weight, in_weight, out_weight):
    return pl.pallas_call(
        prepare_kernel,
        out_shape=(
            jax.ShapeDtypeStruct((LAYERS, 3, BLK * F, 256), BF16),
            jax.ShapeDtypeStruct((EXT * F, 72), BF16),
            jax.ShapeDtypeStruct((OWN, OWN * F), BF16),
        ),
        in_specs=[VMEM] * 3,
        out_specs=(VMEM,) * 3,
        compiler_params=PARAMS,
        cost_estimate=pl.CostEstimate(flops=2_000_000, bytes_accessed=2_000_000, transcendentals=0),
        name="prepare",
    )(conv_weight.transpose(0, 3, 4, 1, 2), in_weight.T, out_weight.reshape(1, F))


def denoise(edge, left, raw, right, flags, band, first, last, table):
    return pl.pallas_call(
        denoise_kernel,
        out_shape=jax.ShapeDtypeStruct((64, 128), BF16),
        in_specs=[SMEM] + [VMEM] * 8,
        out_specs=VMEM,
        scratch_shapes=[
            pltpu.VMEM((3, EXT * F, WIDE), BF16),
            pltpu.VMEM((EXT * F, WIDE), BF16),
            pltpu.VMEM((64, 128), F32),
        ],
        compiler_params=PARAMS,
        name="denoise",
    )(edge, left, raw, right, flags, band, first, last, table)


def turn(rows):
    return pl.pallas_call(
        turn_kernel,
        out_shape=jax.ShapeDtypeStruct((128, 128), BF16),
        in_specs=[VMEM],
        out_specs=VMEM,
        compiler_params=PARAMS,
        name="turn",
    )(rows)


def coherence(half, sources, rows):
    return pl.pallas_call(
        coherence_kernel,
        out_shape=jax.ShapeDtypeStruct((1, 2, 128, 512), F32),
        in_specs=[SMEM, VMEM, VMEM],
        out_specs=VMEM,
        scratch_shapes=[pltpu.VMEM((16, CH_ALL), F32)],
        compiler_params=PARAMS,
        name="coherence",
    )(half, sources.reshape(1, 128), rows)


CHAN = ("y", "z", "c")


def per_device(raw, flags, in_weight, conv_weight, out_weight, sources):
    count = lax.axis_size(CHAN)
    me = lax.axis_index(CHAN)
    left = lax.ppermute(raw, CHAN, [(i, i + 1) for i in range(count - 1)])
    right = lax.ppermute(raw, CHAN, [(i + 1, i) for i in range(count - 1)])
    edge = jnp.stack([me == 0, me == count - 1]).astype(jnp.int32)
    half = lax.axis_index("w").reshape(1).astype(jnp.int32)
    band, first, last = prepare(conv_weight, in_weight, out_weight)
    table = jnp.asarray(dft_table())
    sent = denoise(edge, left, raw, right, flags, band, first, last, table)
    got = lax.all_to_all(sent, "z", 0, 0, tiled=True)
    turned = turn(got)
    mine = lax.all_to_all(turned, ("w", "c", "y", "s"), 0, 0, tiled=True)
    return coherence(half, sources, mine)


def solution(mesh):
    fine = Mesh(mesh.devices.reshape(2, 4, 16, 2, 2), ("s", "y", "z", "c", "w"))
    placed = (P(("s", "w"), CHAN, None), P(("s", "w"), CHAN), P(), P(), P(), P())
    return jax.shard_map(
        per_device,
        mesh=fine,
        in_specs=placed,
        out_specs=P(("s",) + CHAN, None, None, "w"),
        check_vma=False,
    )
```

profile of v0, /device:TPU:1, one launch (start us, length us, event | category | flops | bytes accessed | tf_op | source)
XLA Modules:
  0.0 62.9 jit_solution(1162546749358372129)
XLA Ops:
  0.0 4.9 %collective-permute-start = (bf16[2,8,640]{2,1,0:T(8,128)(2,1)}, bf16[2,8,640]{2,1,0:T(8,128)(2,1)S(1)}, u32[]{:S(2)}, u32[]{:S(2)}) collective-permute-start(bf16[2,8,640]{2,1,0:T(8,128)(2,1)} %raw_ref.1), channel_id=1, source_target_pairs={{0,2},{2,4},{4,6},{6,8},{8,10},{10,12},{12,14},{14,16},{16,18},{18... | collective-permute-start | bytes 61448 | tf_op jit(solution)/shard_map/ppermute | solution.py:274
  4.9 5.1 %collective-permute-start.1 = (bf16[2,8,640]{2,1,0:T(8,128)(2,1)}, bf16[2,8,640]{2,1,0:T(8,128)(2,1)S(1)}, u32[]{:S(2)}, u32[]{:S(2)}) collective-permute-start(bf16[2,8,640]{2,1,0:T(8,128)(2,1)} %raw_ref.1), channel_id=1, source_target_pairs={{2,0},{4,2},{6,4},{8,6},{10,8},{12,10},{14,12},{16,14},{18,16},{20... | collective-permute-start | bytes 61448 | tf_op jit(solution)/shard_map/ppermute | solution.py:275
  10.1 0.1 add_convert_fusion.edge_ref
  10.2 0.0 copy-start.3
  10.2 0.0 copy-start.5
  10.2 0.7 %copy-done.3 = bf16[32,3]{0,1:T(4,128)(2,1)S(1)} copy-done((bf16[32,3]{0,1:T(4,128)(2,1)S(1)}, bf16[32,3]{0,1:T(4,128)(2,1)}, u32[]{:S(2)}) %copy-start.3) | copy-done | bytes 216
  10.9 0.0 copy-done.5
  10.9 0.0 copy-start.1
  10.9 0.9 %copy-done.1 = bf16[3,32,32,3,3]{2,1,4,3,0:T(8,128)(2,1)S(1)} copy-done((bf16[3,32,32,3,3]{2,1,4,3,0:T(8,128)(2,1)S(1)}, bf16[3,32,32,3,3]{2,1,4,3,0:T(8,128)(2,1)}, u32[]{:S(2)}) %copy-start.1) | copy-done | bytes 55320
  11.8 0.0 copy-start.2
  11.8 1.4 %prepare.1 = (bf16[3,3,192,256]{3,2,1,0:T(8,128)(2,1)S(1)}, bf16[448,72]{1,0:T(8,128)(2,1)S(1)}, bf16[8,256]{1,0:T(8,128)(2,1)S(1)}) custom-call(bf16[3,3,3,32,32]{4,3,2,1,0:T(8,128)(2,1)S(1)} %bitcast.11, bf16[3,32]{1,0:T(4,128)(2,1)S(1)} %bitcast.15, bf16[1,32]{1,0:T(2,128)(2,1)S(1)} %bitcast.16), custom_call_target="tpu_custom_call" | custom-call | flops 2000000 | bytes 2000000 | tf_op jit(solution)/shard_map/prepare/pallas_call | solution.py:214
  13.2 0.0 collective-permute-done.left_ref
  13.2 0.0 collective-permute-done.1.right_ref
  13.2 0.0 copy-start.4
  13.3 0.0 copy-done.2
  13.3 0.7 %copy-done.4 = s32[2,8]{1,0:T(2,128)S(1)} copy-done((s32[2,8]{1,0:T(2,128)S(1)}, s32[2,8]{1,0:T(2,128)}, u32[]{:S(2)}) %copy-start.4) | copy-done | bytes 88
  13.9 0.0 copy-start
  13.9 1.1 %copy-done = bf16[640,512]{1,0:T(8,128)(2,1)S(1)} copy-done((bf16[640,512]{1,0:T(8,128)(2,1)S(1)}, bf16[640,512]{1,0:T(8,128)(2,1)}, u32[]{:S(2)}) %copy-start) | copy-done | bytes 655384
  15.0 4.8 %denoise.1 = bf16[64,128]{1,0:T(8,128)(2,1)S(1)} custom-call(s32[2]{0:T(128)S(1)} %add_convert_fusion.edge_ref, bf16[2,8,640]{2,1,0:T(8,128)(2,1)S(1)} %collective-permute-done.left_ref, bf16[2,8,640]{2,1,0:T(8,128)(2,1)S(1)} %copy-done.2, bf16[2,8,640]{2,1,0:T(8,128)(2,1)S(1)} %collective-permute-done.1.right_ref, s32[2,8]{1,0:T(2,128)S(1)} %copy-done.4, ...), custom_call_target="tpu_custom_call" | custom-call | tf_op jit(solution)/shard_map/denoise/pallas_call | solution.py:230
  19.8 23.0 %all_to_all.22 = bf16[16,4,128]{2,1,0:T(4,128)(2,1)S(1)} all-to-all(bf16[16,4,128]{2,1,0:T(4,128)(2,1)S(1)} %bitcast.13), channel_id=1, replica_groups=mesh['s'=2,'y'=4,'z'=16,'c'=2,'w'=2] {'z'}, dimensions={0} | all-to-all | bytes 32768 | tf_op jit(solution)/shard_map/all_to_all | solution.py:281
  42.8 0.9 %turn.1 = bf16[128,128]{1,0:T(8,128)(2,1)} custom-call(bf16[64,128]{1,0:T(8,128)(2,1)S(1)} %bitcast.14), custom_call_target="tpu_custom_call" | custom-call | tf_op jit(solution)/shard_map/turn/pallas_call | solution.py:246
  43.7 9.9 %all-to-all-start.1 = ((bf16[32,4,128]{2,1,0:T(4,128)(2,1)}), bf16[32,4,128]{2,1,0:T(4,128)(2,1)S(1)}, u32[]{:S(2)}, u32[]{:S(2)}) async-start(bf16[32,4,128]{2,1,0:T(4,128)(2,1)} %bitcast.9), calls=%async_computation.1 | async-start | bytes 65536 | tf_op jit(solution)/shard_map/all_to_all | solution.py:283
  53.6 7.3 %all-to-all-done.1 = bf16[32,4,128]{2,1,0:T(4,128)(2,1)S(1)} async-done(((bf16[32,4,128]{2,1,0:T(4,128)(2,1)}), bf16[32,4,128]{2,1,0:T(4,128)(2,1)S(1)}, u32[]{:S(2)}, u32[]{:S(2)}) %all-to-all-start.1) | async-done | bytes 32800 | tf_op jit(solution)/shard_map/all_to_all | solution.py:283
  60.8 0.0 copy-start.6
  60.8 0.7 %copy-done.6 = s32[128]{0:T(128)S(1)} copy-done((s32[128]{0:T(128)S(1)}, s32[128]{0:T(128)}, u32[]{:S(2)}) %copy-start.6) | copy-done | bytes 536
  61.5 1.4 %coherence.1 = f32[1,2,128,512]{3,2,1,0:T(8,128)} custom-call(s32[1]{0:T(128)} %bitcast.half_ref, s32[1,128]{1,0:T(1,128)S(1)} %bitcast.17, bf16[128,128]{1,0:T(8,128)(2,1)S(1)} %bitcast.12), custom_call_target="tpu_custom_call" | custom-call | tf_op jit(solution)/shard_map/coherence/pallas_call | solution.py:257
Async XLA Ops:
  0.0 13.2 %collective-permute-start = (bf16[2,8,640]{2,1,0:T(8,128)(2,1)}, bf16[2,8,640]{2,1,0:T(8,128)(2,1)S(1)}, u32[]{:S(2)}, u32[]{:S(2)}) collective-permute-start(bf16[2,8,640]{2,1,0:T(8,128)(2,1)} %raw_ref.1), channel_id=1, source_target_pairs={{0,2},{2,4},{4,6},{6,8},{8,10},{10,12},{12,14},{14,16},{16,18},{18... | collective-permute-start | bytes 61448 | tf_op jit(solution)/shard_map/ppermute | solution.py:274
  4.9 8.3 %collective-permute-start.1 = (bf16[2,8,640]{2,1,0:T(8,128)(2,1)}, bf16[2,8,640]{2,1,0:T(8,128)(2,1)S(1)}, u32[]{:S(2)}, u32[]{:S(2)}) collective-permute-start(bf16[2,8,640]{2,1,0:T(8,128)(2,1)} %raw_ref.1), channel_id=1, source_target_pairs={{2,0},{4,2},{6,4},{8,6},{10,8},{12,10},{14,12},{16,14},{18,16},{20... | collective-permute-start | bytes 61448 | tf_op jit(solution)/shard_map/ppermute | solution.py:275
  10.2 0.7 %copy-start.3 = (bf16[32,3]{0,1:T(4,128)(2,1)S(1)}, bf16[32,3]{0,1:T(4,128)(2,1)}, u32[]{:S(2)}) copy-start(bf16[32,3]{0,1:T(4,128)(2,1)} %param.9) | copy-start | bytes 580
  10.2 0.7 %copy-start.5 = (bf16[32]{0:T(256)(128)(2,1)S(1)}, bf16[32]{0:T(256)(128)(2,1)}, u32[]{:S(2)}) copy-start(bf16[32]{0:T(256)(128)(2,1)} %param.11) | copy-start | bytes 196
  10.9 0.9 %copy-start.1 = (bf16[3,32,32,3,3]{2,1,4,3,0:T(8,128)(2,1)S(1)}, bf16[3,32,32,3,3]{2,1,4,3,0:T(8,128)(2,1)}, u32[]{:S(2)}) copy-start(bf16[3,32,32,3,3]{2,1,4,3,0:T(8,128)(2,1)} %param.10) | copy-start | bytes 165892
  11.8 1.5 %copy-start.2 = (bf16[2,8,640]{2,1,0:T(8,128)(2,1)S(1)}, bf16[2,8,640]{2,1,0:T(8,128)(2,1)}, u32[]{:S(2)}) copy-start(bf16[2,8,640]{2,1,0:T(8,128)(2,1)} %raw_ref.1) | copy-start | bytes 61444
  13.2 0.7 %copy-start.4 = (s32[2,8]{1,0:T(2,128)S(1)}, s32[2,8]{1,0:T(2,128)}, u32[]{:S(2)}) copy-start(s32[2,8]{1,0:T(2,128)} %flags_ref.1) | copy-start | bytes 196
  13.9 1.1 %copy-start = (bf16[640,512]{1,0:T(8,128)(2,1)S(1)}, bf16[640,512]{1,0:T(8,128)(2,1)}, u32[]{:S(2)}) copy-start(bf16[640,512]{1,0:T(8,128)(2,1)} %constant.27.clone.table_ref) | copy-start | bytes 1966084
  43.7 17.1 %all-to-all-start.1 = ((bf16[32,4,128]{2,1,0:T(4,128)(2,1)}), bf16[32,4,128]{2,1,0:T(4,128)(2,1)S(1)}, u32[]{:S(2)}, u32[]{:S(2)}) async-start(bf16[32,4,128]{2,1,0:T(4,128)(2,1)} %bitcast.9), calls=%async_computation.1 | async-start | bytes 65536 | tf_op jit(solution)/shard_map/all_to_all | solution.py:283
  60.8 0.7 %copy-start.6 = (s32[128]{0:T(128)S(1)}, s32[128]{0:T(128)}, u32[]{:S(2)}) copy-start(s32[128]{0:T(128)} %param.12) | copy-start | bytes 1540
where the time goes:
time: 63.2 us; the launch traced here: 62.9 us
  blocking collectives  23 us (36%)
  starting transfers between devices  19.9 us (31%)
  Pallas kernels  8.51 us (13%)
  waiting for transfers between devices  7.27 us (12%)
  local copies, waits for them, and re-layouts  4.03 us (6%)
    all_to_all x1, blocking collectives, per_device(): got = lax.all_to_all(sent, 'z', 0, 0, tiled=True)  23 us
    all_to_all x1, starting transfers between devices, per_device(): mine = lax.all_to_all(turned, ('w', 'c', 'y', 's'), 0, 0, tiled=True)  9.86 us
    all_to_all x1, waiting for transfers between devices, per_device(): mine = lax.all_to_all(turned, ('w', 'c', 'y', 's'), 0, 0, tiled=True)  7.26 us
    ppermute x1, starting transfers between devices, per_device(): right = lax.ppermute(raw, CHAN, [(i + 1, i) for i in range(count - 1)])  5.14 us
    ppermute x1, starting transfers between devices, per_device(): left = lax.ppermute(raw, CHAN, [(i, i + 1) for i in range(count - 1)])  4.93 us
    pallas_call x1, Pallas kernels, denoise(): pl.pallas_call(denoise_kernel, out_shape=jax.ShapeDtypeStruct((64, 128),...  4.79 us
    unnamed x14, local copies, waits for them, and re-layouts  4.03 us
    pallas_call x1, Pallas kernels, prepare(): pl.pallas_call(prepare_kernel, out_shape=(jax.ShapeDtypeStruct((LAYERS, 3...  1.42 us
  transfers between devices with their start and end apart: 3, of which 1 were waited for; matrix products, arithmetic and copies ran while one was open for 0% of the time, Pallas kernels for 2%

commit v1 on v0

--- a/solution.py
+++ b/solution.py
@@ -56,14 +56,19 @@
     return jnp.where(row_bit == lane_bit, x, jnp.where(row_bit == 0, down, up))
 
 
-def prepare_kernel(conv_ref, in_ref, out_ref, band_ref, first_ref, last_ref):
-    for layer in range(LAYERS):
-        for tap in range(3):
-            taps = [conv_ref[layer, a, tap].astype(F32) for a in range(3)]
-            base = jnp.concatenate(taps + [jnp.zeros((F, 256 - 3 * F), F32)], axis=1)
-            for c in range(BLK):
-                row = base if c == 0 else pltpu.roll(base, F * c, 1)
-                band_ref[layer, tap, F * c : F * (c + 1), :] = row.astype(BF16)
+def prepare_kernel(
+    conv_any, in_any, out_any, table_any, raw_any, flags_any, sources_any,
+    band_ref, first_ref, last_ref, table_ref, raw_ref, flags_ref, sources_ref,
+    conv_ref, in_ref, out_ref, sems,
+):
+    pairs = (
+        (conv_any, conv_ref), (in_any, in_ref), (out_any, out_ref), (raw_any, raw_ref),
+        (flags_any, flags_ref), (sources_any, sources_ref), (table_any, table_ref),
+    )
+    copies = [pltpu.make_async_copy(a, b, sems.at[i]) for i, (a, b) in enumerate(pairs)]
+    for copy in copies:
+        copy.start()
+    copies[1].wait()
     shape = (EXT * F, 72)
     channel = iota(shape, 0) // F
     place = jnp.where(channel < 3, 13 + channel, jnp.where(channel < 11, channel - 3, channel + 5))
@@ -74,11 +79,22 @@
         tall = jnp.broadcast_to(jnp.concatenate([weight] * EXT, axis=0), shape)
         first = jnp.where(lane == place + 24 * tap, tall, first)
     first_ref[...] = first.astype(BF16)
+    copies[2].wait()
     shape = (OWN, OWN * F)
     wide = jnp.concatenate([out_ref[...].astype(F32)] * OWN, axis=1)
     last_ref[...] = jnp.where(
         iota(shape, 0) == iota(shape, 1) // F, jnp.broadcast_to(wide, shape), 0.0
     ).astype(BF16)
+    copies[0].wait()
+    for layer in range(LAYERS):
+        for tap in range(3):
+            taps = [conv_ref[layer, a, tap] for a in range(3)]
+            base = jnp.concatenate(taps + [jnp.zeros((F, 256 - 3 * F), BF16)], axis=1)
+            for c in range(BLK):
+                row = base if c == 0 else pltpu.roll(base, F * c, 1)
+                band_ref[layer, F * c : F * (c + 1), 256 * tap : 256 * (tap + 1)] = row
+    for copy in copies[3:]:
+        copy.wait()
 
 
 def shifted(x, step):
@@ -89,53 +105,72 @@
 
 
 def denoise_kernel(
-    edge_ref, left_ref, raw_ref, right_ref, flags_ref, band_ref, first_ref, last_ref, table_ref,
-    out_ref, taps_ref, next_ref, line_ref,
+    edge_ref, near_ref, raw_ref, far_ref, flags_ref, band_ref, first_ref, last_ref, table_ref,
+    out_ref, h0_ref, h1_ref, h2_ref, h3_ref, taps_ref, line_ref,
 ):
-    is_first, is_last = edge_ref[0], edge_ref[1]
+    is_first, is_last, odd = edge_ref[0], edge_ref[1], edge_ref[2]
+    own, near, far = (
+        jnp.concatenate([ref[w].astype(F32) for w in range(WIN)], axis=1)
+        for ref in (raw_ref, near_ref, far_ref)
+    )
     rows = jnp.concatenate(
-        [
-            jnp.concatenate([ref[w].astype(F32) for w in range(WIN)], axis=1)
-            for ref in (raw_ref, left_ref, right_ref)
-        ],
-        axis=0,
+        [own, jnp.where(odd == 1, near, far), jnp.where(odd == 1, far, near)], axis=0
     )
     lines = jnp.concatenate([shifted(rows, 1), rows, shifted(rows, -1)], axis=0).astype(BF16)
-    for n in range(0, WIDE, 256):
-        next_ref[:, n : n + 256] = jnp.dot(
-            first_ref[...], lines[:, n : n + 256], preferred_element_type=F32
+    hidden = (h0_ref, h1_ref, h2_ref, h3_ref)
+
+    def input_chunk(n):
+        h0_ref[:, n * 256 : (n + 1) * 256] = jnp.dot(
+            first_ref[...], lines[:, n * 256 : (n + 1) * 256], preferred_element_type=F32
         ).astype(BF16)
-    count = EXT
-    for layer in range(LAYERS):
+
+    def taps_column(layer, j):
         step = 2**layer
-        for r in range(0, count * F, F):
-            block = next_ref[r : r + F, :].astype(F32)
-            taps_ref[0, r : r + F, :] = shifted(block, step).astype(BF16)
-            taps_ref[1, r : r + F, :] = next_ref[r : r + F, :]
-            taps_ref[2, r : r + F, :] = shifted(block, -step).astype(BF16)
-        count -= 2
-        for c in range(0, count, BLK):
-            size = min(BLK, count - c)
-            for n in range(0, WIDE, 256):
-                total = None
-                for tap in range(3):
-                    term = jnp.dot(
-                        band_ref[layer, tap, : size * F, : (size + 2) * F],
-                        taps_ref[tap, c * F : (c + size + 2) * F, n : n + 256],
-                        preferred_element_type=F32,
-                    )
-                    total = term if total is None else total + term
-                old = taps_ref[1, (c + 1) * F : (c + 1 + size) * F, n : n + 256].astype(F32)
-                new = old + jnp.maximum(total, 0.0)
-                reach = LAYERS - 1 - layer
-                for k in range(size):
-                    part = new[k * F : (k + 1) * F]
-                    if c + k < reach:
-                        part = jnp.where(is_first == 1, 0.0, part)
-                    if c + k >= count - reach:
-                        part = jnp.where(is_last == 1, 0.0, part)
-                    next_ref[(c + k) * F : (c + k + 1) * F, n : n + 256] = part.astype(BF16)
-    clean = jnp.dot(last_ref[...], next_ref[: OWN * F, :], preferred_element_type=F32)
+        source = hidden[layer]
+        size = (EXT - 2 * layer) * F
+        lane = iota((size, 128), 1)
+        here = source[:, j * 128 : (j + 1) * 128]
+        zero = jnp.zeros_like(here)
+        inside = j % 5
+        before = zero if inside == 0 else pltpu.roll(source[:, (j - 1) * 128 : j * 128], step, 1)
+        taps_ref[0, :size, j * 128 : (j + 1) * 128] = jnp.where(
+            lane < step, before, pltpu.roll(here, step, 1)
+        )
+        after = zero if inside == 4 else pltpu.roll(source[:, (j + 1) * 128 : (j + 2) * 128], 128 - step, 1)
+        taps_ref[1, :size, j * 128 : (j + 1) * 128] = jnp.where(
+            lane >= 128 - step, after, pltpu.roll(here, 128 - step, 1)
+        )
+
+    def layer_chunk(layer, n):
+        source, target = hidden[layer], hidden[layer + 1]
+        count = EXT - 2 * (layer + 1)
+        reach = LAYERS - 1 - layer
+        cols = slice(n * 256, (n + 1) * 256)
+        taps_column(layer, 2 * n)
+        taps_column(layer, 2 * n + 1)
+        for start, low in ((0, 0), (count - BLK, 2 * BLK - count)):
+            k = slice(start * F, (start + BLK + 2) * F)
+            window = jnp.concatenate([taps_ref[0, k, cols], source[k, cols], taps_ref[1, k, cols]], axis=0)
+            total = jnp.dot(band_ref[layer, low * F :, :], window, preferred_element_type=F32)
+            old = source[(start + low + 1) * F : (start + BLK + 1) * F, cols].astype(F32)
+            new = old + jnp.maximum(total, 0.0)
+            for i in range(BLK - low):
+                c = start + low + i
+                part = new[i * F : (i + 1) * F]
+                if c < reach:
+                    part = jnp.where(is_first == 1, 0.0, part)
+                if c >= count - reach:
+                    part = jnp.where(is_last == 1, 0.0, part)
+                target[c * F : (c + 1) * F, cols] = part.astype(BF16)
+
+    chunks = WIDE // 256
+    for n in range(chunks + LAYERS):
+        if n < chunks:
+            input_chunk(n)
+        for layer in range(LAYERS):
+            if 0 <= n - layer - 1 < chunks:
+                layer_chunk(layer, n - layer - 1)
+    clean = jnp.dot(last_ref[...], h3_ref[...], preferred_element_type=F32)
     clean = jnp.concatenate([clean[:, w * NT : (w + 1) * NT] for w in range(WIN)], axis=0)
     spectra = jnp.dot(clean.astype(BF16), table_ref[...], preferred_element_type=F32)
     real, imag = spectra[:, :NF], spectra[:, NF:]
@@ -164,7 +199,7 @@
     out_ref[64:, :] = x
 
 
-def coherence_kernel(half_ref, sources_ref, in_ref, out_ref, all_ref):
+def coherence_kernel(half_ref, sources_ref, in_ref, out_any, all_ref, out_ref, sems):
     x = in_ref[...].astype(F32)
 
     def piece(w, c, y):
@@ -199,8 +234,13 @@
     energy_rec = jnp.sum(receivers * receivers, axis=0, keepdims=True)
     scale = lax.rsqrt(jnp.maximum(energy_src * energy_rec, 1.0))
     left = chosen_t.astype(BF16)
-    out_ref[0, 0] = jnp.dot(left, receivers.astype(BF16), preferred_element_type=F32) * scale
-    out_ref[0, 1] = jnp.dot(left, turned.astype(BF16), preferred_element_type=F32) * scale
+    copies = []
+    for part, right in enumerate((receivers, turned)):
+        out_ref[part] = jnp.dot(left, right.astype(BF16), preferred_element_type=F32) * scale
+        copies.append(pltpu.make_async_copy(out_ref.at[part], out_any.at[0, part], sems.at[part]))
+        copies[-1].start()
+    for copy in copies:
+        copy.wait()
 
 
 CH_ALL = 1024
@@ -210,36 +250,41 @@
 PARAMS = pltpu.CompilerParams(vmem_limit_bytes=32 * 1024 * 1024)
 
 
-def prepare(conv_weight, in_weight, out_weight):
+def prepare(conv_weight, in_weight, out_weight, table, raw, flags, sources):
+    arrays = (
+        conv_weight.transpose(0, 3, 4, 1, 2), in_weight.T, out_weight.reshape(1, F),
+        table, raw, flags, sources.reshape(1, -1),
+    )
+    arrays = tuple(pltpu.with_memory_space_constraint(a, pltpu.HBM) for a in arrays)
     return pl.pallas_call(
         prepare_kernel,
         out_shape=(
-            jax.ShapeDtypeStruct((LAYERS, 3, BLK * F, 256), BF16),
+            jax.ShapeDtypeStruct((LAYERS, BLK * F, 3 * 256), BF16),
             jax.ShapeDtypeStruct((EXT * F, 72), BF16),
             jax.ShapeDtypeStruct((OWN, OWN * F), BF16),
-        ),
-        in_specs=[VMEM] * 3,
-        out_specs=(VMEM,) * 3,
+        )
+        + tuple(jax.ShapeDtypeStruct(a.shape, a.dtype) for a in arrays[3:]),
+        in_specs=[pl.BlockSpec(memory_space=pl.ANY)] * 7,
+        out_specs=(VMEM,) * 7,
+        scratch_shapes=[pltpu.VMEM(a.shape, a.dtype) for a in arrays[:3]]
+        + [pltpu.SemaphoreType.DMA((7,))],
         compiler_params=PARAMS,
-        cost_estimate=pl.CostEstimate(flops=2_000_000, bytes_accessed=2_000_000, transcendentals=0),
+        cost_estimate=pl.CostEstimate(flops=2_000_000, bytes_accessed=4_000_000, transcendentals=0),
         name="prepare",
-    )(conv_weight.transpose(0, 3, 4, 1, 2), in_weight.T, out_weight.reshape(1, F))
-
-
-def denoise(edge, left, raw, right, flags, band, first, last, table):
+    )(*arrays)
+
+
+def denoise(edge, near, raw, far, flags, band, first, last, table):
     return pl.pallas_call(
         denoise_kernel,
         out_shape=jax.ShapeDtypeStruct((64, 128), BF16),
         in_specs=[SMEM] + [VMEM] * 8,
         out_specs=VMEM,
-        scratch_shapes=[
-            pltpu.VMEM((3, EXT * F, WIDE), BF16),
-            pltpu.VMEM((EXT * F, WIDE), BF16),
-            pltpu.VMEM((64, 128), F32),
-        ],
+        scratch_shapes=[pltpu.VMEM(((EXT - 2 * i) * F, WIDE), BF16) for i in range(LAYERS + 1)]
+        + [pltpu.VMEM((2, EXT * F, WIDE), BF16), pltpu.VMEM((64, 128), F32)],
         compiler_params=PARAMS,
         name="denoise",
-    )(edge, left, raw, right, flags, band, first, last, table)
+    )(edge, near, raw, far, flags, band, first, last, table)
 
 
 def turn(rows):
@@ -258,11 +303,15 @@
         coherence_kernel,
         out_shape=jax.ShapeDtypeStruct((1, 2, 128, 512), F32),
         in_specs=[SMEM, VMEM, VMEM],
-        out_specs=VMEM,
-        scratch_shapes=[pltpu.VMEM((16, CH_ALL), F32)],
+        out_specs=pl.BlockSpec(memory_space=pl.ANY),
+        scratch_shapes=[
+            pltpu.VMEM((16, CH_ALL), F32),
+            pltpu.VMEM((2, 128, 512), F32),
+            pltpu.SemaphoreType.DMA((2,)),
+        ],
         compiler_params=PARAMS,
         name="coherence",
-    )(half, sources.reshape(1, 128), rows)
+    )(half, sources, rows)
 
 
 CHAN = ("y", "z", "c")
@@ -271,16 +320,19 @@
 def per_device(raw, flags, in_weight, conv_weight, out_weight, sources):
     count = lax.axis_size(CHAN)
     me = lax.axis_index(CHAN)
-    left = lax.ppermute(raw, CHAN, [(i, i + 1) for i in range(count - 1)])
-    right = lax.ppermute(raw, CHAN, [(i + 1, i) for i in range(count - 1)])
-    edge = jnp.stack([me == 0, me == count - 1]).astype(jnp.int32)
+    odd = lax.axis_index("c")
+    across = [(i, i + 1) for i in range(1, count - 1, 2)]
+    far = lax.ppermute(raw, CHAN, across + [(b, a) for a, b in across])
+    near = lax.ppermute(raw, "c", [(0, 1), (1, 0)])
+    edge = jnp.stack([me == 0, me == count - 1, odd == 1]).astype(jnp.int32)
     half = lax.axis_index("w").reshape(1).astype(jnp.int32)
-    band, first, last = prepare(conv_weight, in_weight, out_weight)
-    table = jnp.asarray(dft_table())
-    sent = denoise(edge, left, raw, right, flags, band, first, last, table)
+    band, first, last, table, raw, flags, sources = prepare(
+        conv_weight, in_weight, out_weight, jnp.asarray(dft_table()), raw, flags, sources
+    )
+    sent = denoise(edge, near, raw, far, flags, band, first, last, table)
+    half, sources, sent = lax.optimization_barrier((half, sources, sent))
     got = lax.all_to_all(sent, "z", 0, 0, tiled=True)
-    turned = turn(got)
-    mine = lax.all_to_all(turned, ("w", "c", "y", "s"), 0, 0, tiled=True)
+    mine = lax.all_to_all(turn(got), ("w", "c", "y", "s"), 0, 0, tiled=True)
     return coherence(half, sources, mine)
 
 

time: 63.2 us -> 59.8 us (0.946)
  blocking collectives: 23 us -> 37.5 us
  starting transfers between devices: 19.9 us -> 10.7 us
  waiting for transfers between devices: 7.27 us -> 1.9 us
  local copies, waits for them, and re-layouts: 4.03 us -> 0 us
  Pallas kernels: 8.51 us -> 9.32 us
    all_to_all x0 -> x1, blocking collectives: none -> 16.5 us  [per_device(): mine = lax.all_to_all(turn(got), ('w', 'c', 'y', 's'), 0, 0, tiled=True)]
    all_to_all x1 -> x0, starting transfers between devices: 9.86 us -> none  [per_device(): mine = lax.all_to_all(turned, ('w', 'c', 'y', 's'), 0, 0, tiled=True)]
    all_to_all x1 -> x0, waiting for transfers between devices: 7.26 us -> none  [per_device(): mine = lax.all_to_all(turned, ('w', 'c', 'y', 's'), 0, 0, tiled=True)]
    unnamed x14 -> x0, local copies, waits for them, and re-layouts: 4.03 us -> none
    all_to_all x1, blocking collectives: 23 us -> 21 us  [per_device(): got = lax.all_to_all(sent, 'z', 0, 0, tiled=True)]
    ppermute x2, waiting for transfers between devices: 0.01 us -> 1.9 us  [the longest x1 1.9 us: per_device(): far = lax.ppermute(raw, CHAN, across + [(b, a) for a, b in across])]
    pallas_call x1, Pallas kernels: 4.79 us -> 6.28 us  [denoise(): pl.pallas_call(denoise_kernel, out_shape=jax.ShapeDtypeStruct((64, 128),...]
  transfers between devices with their start and end apart: 3 -> 2, of which waited for: 1 -> 1; matrix products, arithmetic and copies ran while one was open for 0% -> 0% of each run, Pallas kernels for 2% -> 2%
where the time goes in v1:
time: 59.8 us; the launch traced here: 59.5 us
  blocking collectives  37.5 us (63%)
  starting transfers between devices  10.7 us (18%)
  Pallas kernels  9.32 us (16%)
  waiting for transfers between devices  1.9 us (3%)
    all_to_all x1, blocking collectives, per_device(): got = lax.all_to_all(sent, 'z', 0, 0, tiled=True)  21 us
    all_to_all x1, blocking collectives, per_device(): mine = lax.all_to_all(turn(got), ('w', 'c', 'y', 's'), 0, 0, tiled=True)  16.5 us
    ppermute x1, starting transfers between devices, per_device(): near = lax.ppermute(raw, 'c', [(0, 1), (1, 0)])  8.78 us
    pallas_call x1, Pallas kernels, denoise(): pl.pallas_call(denoise_kernel, out_shape=jax.ShapeDtypeStruct((64, 128),...  6.28 us
    ppermute x1, starting transfers between devices, per_device(): far = lax.ppermute(raw, CHAN, across + [(b, a) for a, b in across])  1.92 us
    ppermute x1, waiting for transfers between devices, per_device(): far = lax.ppermute(raw, CHAN, across + [(b, a) for a, b in across])  1.9 us
    pallas_call x1, Pallas kernels, prepare(): pl.pallas_call(prepare_kernel, out_shape=(jax.ShapeDtypeStruct((LAYERS, B...  1.38 us
    pallas_call x1, Pallas kernels, coherence(): pl.pallas_call(coherence_kernel, out_shape=jax.ShapeDtypeStruct((1, 2, 12...  1.36 us
  transfers between devices with their start and end apart: 2, of which 1 were waited for; matrix products, arithmetic and copies ran while one was open for 0% of the time, Pallas kernels for 2%

profile of v1, /device:TPU:1, one launch (start us, length us, event | category | flops | bytes accessed | tf_op | source)
XLA Modules:
  0.0 59.5 jit_solution(16373987444796963417)
XLA Ops:
  0.0 8.8 %collective-permute-start = (bf16[2,8,640]{2,1,0:T(8,128)(2,1)}, bf16[2,8,640]{2,1,0:T(8,128)(2,1)S(1)}, u32[]{:S(2)}, u32[]{:S(2)}) collective-permute-start(bf16[2,8,640]{2,1,0:T(8,128)(2,1)} %raw_any.1), channel_id=1, source_target_pairs={{0,2},{2,0},{1,3},{3,1},{4,6},{6,4},{5,7},{7,5},{8,10},{10,8},{9,1... | collective-permute-start | bytes 61448 | tf_op jit(solution)/shard_map/ppermute | solution.py:326
  8.8 1.9 %collective-permute-start.1 = (bf16[2,8,640]{2,1,0:T(8,128)(2,1)}, bf16[2,8,640]{2,1,0:T(8,128)(2,1)S(1)}, u32[]{:S(2)}, u32[]{:S(2)}) collective-permute-start(bf16[2,8,640]{2,1,0:T(8,128)(2,1)} %raw_any.1), channel_id=1, source_target_pairs={{2,4},{6,8},{10,12},{14,16},{18,20},{22,24},{26,28},{30,32},{34,36... | collective-permute-start | bytes 61448 | tf_op jit(solution)/shard_map/ppermute | solution.py:325
  10.7 0.1 add_convert_fusion.edge_ref
  10.8 1.4 %prepare.1 = (bf16[3,192,768]{2,1,0:T(8,128)(2,1)S(1)}, bf16[448,72]{1,0:T(8,128)(2,1)S(1)}, bf16[8,256]{1,0:T(8,128)(2,1)S(1)}, bf16[640,512]{1,0:T(8,128)(2,1)...) custom-call(bf16[3,3,3,32,32]{4,3,2,1,0:T(8,128)(2,1)} %bitcast.16, ...), custom_call_target="tpu_custom_call" | custom-call | flops 2000000 | bytes 4000000 | tf_op jit(solution)/shard_map/prepare/pallas_call | solution.py:259
  12.2 0.0 collective-permute-done.near_ref
  12.2 1.9 %collective-permute-done.1.far_ref = bf16[2,8,640]{2,1,0:T(8,128)(2,1)S(1)} collective-permute-done((bf16[2,8,640]{2,1,0:T(8,128)(2,1)}, bf16[2,8,640]{2,1,0:T(8,128)(2,1)S(1)}, u32[]{:S(2)}, u32[]{:S(2)}) %collective-permute-start.1) | collective-permute-done | bytes 20512 | tf_op jit(solution)/shard_map/ppermute | solution.py:325
  14.1 6.3 %denoise.1 = bf16[64,128]{1,0:T(8,128)(2,1)S(1)} custom-call(s32[3]{0:T(128)S(1)} %add_convert_fusion.edge_ref, bf16[2,8,640]{2,1,0:T(8,128)(2,1)S(1)} %collective-permute-done.near_ref, bf16[2,8,640]{2,1,0:T(8,128)(2,1)S(1)} %get-tuple-element.16.raw_ref, bf16[2,8,640]{2,1,0:T(8,128)(2,1)S(1)} %collective-permute-done.1.far_ref, ...), custom_call_target="tpu_custom_call" | custom-call | tf_op jit(solution)/shard_map/denoise/pallas_call | solution.py:278
  20.4 21.0 %all_to_all.22 = bf16[16,4,128]{2,1,0:T(4,128)(2,1)S(1)} all-to-all(bf16[16,4,128]{2,1,0:T(4,128)(2,1)S(1)} %bitcast.14), channel_id=1, replica_groups=mesh['s'=2,'y'=4,'z'=16,'c'=2,'w'=2] {'z'}, dimensions={0} | all-to-all | bytes 32768 | tf_op jit(solution)/shard_map/all_to_all | solution.py:334
  41.4 0.3 turn.1
  41.7 16.5 %all_to_all.23 = bf16[32,4,128]{2,1,0:T(4,128)(2,1)S(1)} all-to-all(bf16[32,4,128]{2,1,0:T(4,128)(2,1)S(1)} %bitcast.13), channel_id=1, replica_groups=mesh['s'=2,'y'=4,'z'=16,'c'=2,'w'=2] {'w','c','y','s'}, dimensions={0} | all-to-all | bytes 65536 | tf_op jit(solution)/shard_map/all_to_all | solution.py:335
  58.2 1.4 %coherence.1 = f32[1,2,128,512]{3,2,1,0:T(8,128)} custom-call(s32[1]{0:T(128)} %bitcast.half_ref, s32[1,128]{1,0:T(1,128)S(1)} %get-tuple-element.23.sources_ref, bf16[128,128]{1,0:T(8,128)(2,1)S(1)} %bitcast.12), custom_call_target="tpu_custom_call" | custom-call | tf_op jit(solution)/shard_map/coherence/pallas_call | solution.py:302
Async XLA Ops:
  0.0 12.2 %collective-permute-start = (bf16[2,8,640]{2,1,0:T(8,128)(2,1)}, bf16[2,8,640]{2,1,0:T(8,128)(2,1)S(1)}, u32[]{:S(2)}, u32[]{:S(2)}) collective-permute-start(bf16[2,8,640]{2,1,0:T(8,128)(2,1)} %raw_any.1), channel_id=1, source_target_pairs={{0,2},{2,0},{1,3},{3,1},{4,6},{6,4},{5,7},{7,5},{8,10},{10,8},{9,1... | collective-permute-start | bytes 61448 | tf_op jit(solution)/shard_map/ppermute | solution.py:326
  8.8 5.3 %collective-permute-start.1 = (bf16[2,8,640]{2,1,0:T(8,128)(2,1)}, bf16[2,8,640]{2,1,0:T(8,128)(2,1)S(1)}, u32[]{:S(2)}, u32[]{:S(2)}) collective-permute-start(bf16[2,8,640]{2,1,0:T(8,128)(2,1)} %raw_any.1), channel_id=1, source_target_pairs={{2,4},{6,8},{10,12},{14,16},{18,20},{22,24},{26,28},{30,32},{34,36... | collective-permute-start | bytes 61448 | tf_op jit(solution)/shard_map/ppermute | solution.py:325

commit v2 on v1

v2 whole, which is shorter than its diff:
```python
import functools
import math

import jax
import jax.numpy as jnp
import numpy as np
from jax import lax
from jax.experimental import pallas as pl
from jax.experimental.pallas import tpu as pltpu
from jax.sharding import Mesh, PartitionSpec as P

NT = 640
F = 32
LAYERS = 3
NF = 256
OWN = 8
WIN = 2
EXT = OWN + 2 * LAYERS
BLK = 6
LANES = 128
PH = NT // LANES
CHUNK = WIN * LANES
WIDE = WIN * NT
CH_ALL = 1024
NV = 128

water_level = 0.2
epsilon_power = 1e-06

F32 = jnp.float32
BF16 = jnp.bfloat16


def dft_table():
    part, z, core, y, section = np.meshgrid(
        np.arange(2), np.arange(16), np.arange(2), np.arange(4), np.arange(2), indexing="ij"
    )
    k = (section * 128 + (y * 16 + z) * 2 + core).reshape(-1)
    part = part.reshape(-1)
    phases = np.arange(NT)[:, None] * (k + 1)[None, :] % NT
    angles = phases.astype(np.float32) * np.float32(2.0 * math.pi / NT)
    table = np.where(part[None, :] == 0, np.cos(angles), -np.sin(angles))
    return table[sample_order()].astype(BF16)


def sample_order():
    return (np.arange(LANES)[None, :] * PH + np.arange(PH)[:, None]).reshape(-1)


def sample_perm():
    return np.eye(NT, dtype=np.float32)[:, sample_order()].astype(BF16)


def channel_perm():
    core, channel, z = np.meshgrid(np.arange(2), np.arange(OWN), np.arange(16), indexing="ij")
    target = ((z * 2 + core) * OWN + channel).reshape(-1)
    return np.eye(256, dtype=np.float32)[target].astype(BF16)


def iota(shape, dim):
    return lax.broadcasted_iota(jnp.int32, shape, dim)


def column(row, n):
    eye = iota((n, n), 0) == iota((n, n), 1)
    return jnp.sum(jnp.where(eye, jnp.broadcast_to(row, (n, n)), 0.0), axis=1, keepdims=True)


def swap_bits(x, row_step, lane_step):
    rows, lanes = x.shape
    row_bit = (iota(x.shape, 0) // row_step) % 2
    lane_bit = (iota(x.shape, 1) // lane_step) % 2
    down = pltpu.roll(pltpu.roll(x, rows - row_step, 0), lane_step, 1)
    up = pltpu.roll(pltpu.roll(x, row_step, 0), lanes - lane_step, 1)
    return jnp.where(row_bit == lane_bit, x, jnp.where(row_bit == 0, down, up))


def prepare_kernel(
    conv_any, in_any, out_any, sources_any, raw_any, flags_any, order_any, table_any, perm_any,
    band_ref, first_ref, last_ref, one_hot_ref, raw_ref, flags_ref, order_ref, table_ref, perm_ref,
    conv_ref, in_ref, out_ref, sources_ref, sems,
):
    pairs = (
        (conv_any, conv_ref), (in_any, in_ref), (out_any, out_ref), (sources_any, sources_ref),
        (raw_any, raw_ref), (flags_any, flags_ref), (order_any, order_ref), (table_any, table_ref),
        (perm_any, perm_ref),
    )
    copies = [pltpu.make_async_copy(a, b, sems.at[i]) for i, (a, b) in enumerate(pairs)]
    for copy in copies:
        copy.start()
    copies[1].wait()
    shape = (EXT * F, 72)
    channel = iota(shape, 0) // F
    place = jnp.where(channel < 3, 13 + channel, jnp.where(channel < 11, channel - 3, channel + 5))
    lane = iota(shape, 1)
    first = jnp.zeros(shape, F32)
    for tap in range(3):
        weight = column(in_ref[tap : tap + 1, :].astype(F32), F)
        tall = jnp.broadcast_to(jnp.concatenate([weight] * EXT, axis=0), shape)
        first = jnp.where(lane == place + 24 * tap, tall, first)
    first_ref[...] = first.astype(BF16)
    copies[2].wait()
    shape = (OWN, OWN * F)
    wide = jnp.concatenate([out_ref[...].astype(F32)] * OWN, axis=1)
    last_ref[...] = jnp.where(
        iota(shape, 0) == iota(shape, 1) // F, jnp.broadcast_to(wide, shape), 0.0
    ).astype(BF16)
    copies[3].wait()
    shape = (CH_ALL, NV)
    one_hot_ref[...] = jnp.where(
        iota(shape, 0) == jnp.broadcast_to(sources_ref[...], shape), 1.0, 0.0
    ).astype(BF16)
    copies[0].wait()
    for layer in range(LAYERS):
        for tap in range(3):
            taps = [conv_ref[layer, a, tap] for a in range(3)]
            base = jnp.concatenate(taps + [jnp.zeros((F, 256 - 3 * F), BF16)], axis=1)
            for c in range(BLK):
                row = base if c == 0 else pltpu.roll(base, F * c, 1)
                band_ref[layer, F * c : F * (c + 1), 256 * tap : 256 * (tap + 1)] = row
    for copy in copies[4:]:
        copy.wait()


def lane_shift(x, step):
    edge = iota((x.shape[0], LANES), 1) == (0 if step == 1 else LANES - 1)
    moved = [
        jnp.where(edge, jnp.zeros_like(part), pltpu.roll(part, step % LANES, 1))
        for part in (x[:, i : i + LANES] for i in range(0, x.shape[1], LANES))
    ]
    return jnp.concatenate(moved, axis=1)


def denoise_kernel(
    edge_ref, near_ref, raw_ref, far_ref, flags_ref, order_ref, band_ref, first_ref, last_ref, table_ref,
    out_ref, h0_ref, h1_ref, h2_ref, h3_ref, earlier_ref, later_ref, line_ref,
):
    is_first, is_last, odd = edge_ref[0], edge_ref[1], edge_ref[2]
    near, far = near_ref[...].astype(F32), far_ref[...].astype(F32)
    left, right = jnp.where(odd == 1, near, far), jnp.where(odd == 1, far, near)
    rows = [x for w in range(WIN) for x in (raw_ref[w].astype(F32), left[w], right[w])]
    rows = jnp.concatenate(rows, axis=0).astype(BF16)
    rows = jnp.dot(rows, order_ref[...], preferred_element_type=F32)
    lines = [
        jnp.concatenate(
            [rows[24 * w : 24 * (w + 1), v * LANES : (v + 1) * LANES] for w in range(WIN)], axis=1
        )
        for v in range(PH)
    ]
    hidden = (h0_ref, h1_ref, h2_ref, h3_ref)
    chunk = [slice(v * CHUNK, (v + 1) * CHUNK) for v in range(PH)]
    for v in range(PH):
        before = lines[v - 1] if v > 0 else lane_shift(lines[PH - 1], 1)
        after = lines[v + 1] if v < PH - 1 else lane_shift(lines[0], -1)
        taps = jnp.concatenate([before, lines[v], after], axis=0).astype(BF16)
        h0_ref[:, chunk[v]] = jnp.dot(first_ref[...], taps, preferred_element_type=F32).astype(BF16)
    for layer in range(LAYERS):
        step = 2**layer
        source, target = hidden[layer], hidden[layer + 1]
        size = (EXT - 2 * layer) * F
        count = EXT - 2 * (layer + 1)
        reach = LAYERS - 1 - layer
        for v in sorted(range(PH), key=lambda v: (v < step) + (v >= PH - step)):
            before, after, u, t = source, source, v - step, v + step
            if u < 0:
                u += PH
                before = earlier_ref
                earlier_ref[:size, chunk[u]] = lane_shift(source[:, chunk[u]], 1)
            if t >= PH:
                t -= PH
                after = later_ref
                later_ref[:size, chunk[t]] = lane_shift(source[:, chunk[t]], -1)
            for start, low in ((0, 0), (count - BLK, 2 * BLK - count)):
                k = slice(start * F, (start + BLK + 2) * F)
                taps = jnp.concatenate([before[k, chunk[u]], source[k, chunk[v]], after[k, chunk[t]]], axis=0)
                total = jnp.dot(band_ref[layer, low * F :, :], taps, preferred_element_type=F32)
                old = source[(start + low + 1) * F : (start + BLK + 1) * F, chunk[v]].astype(F32)
                new = old + jnp.maximum(total, 0.0)
                for i in range(BLK - low):
                    c = start + low + i
                    part = new[i * F : (i + 1) * F]
                    if c < reach:
                        part = jnp.where(is_first == 1, 0.0, part)
                    if c >= count - reach:
                        part = jnp.where(is_last == 1, 0.0, part)
                    target[c * F : (c + 1) * F, chunk[v]] = part.astype(BF16)
    clean = jnp.dot(last_ref[...], h3_ref[...], preferred_element_type=F32)
    clean = jnp.concatenate(
        [
            jnp.concatenate(
                [clean[:, v * CHUNK + w * LANES : v * CHUNK + (w + 1) * LANES] for v in range(PH)], axis=1
            )
            for w in range(WIN)
        ],
        axis=0,
    )
    spectra = jnp.dot(clean.astype(BF16), table_ref[...], preferred_element_type=F32)
    real, imag = spectra[:, :NF], spectra[:, NF:]
    power = real * real + imag * imag
    spread = jnp.sqrt(jnp.mean(power, axis=1, keepdims=True) + epsilon_power)
    flags = jnp.concatenate(
        [column(flags_ref[w : w + 1, :].astype(F32), OWN) for w in range(WIN)], axis=0
    )
    factor = flags / (jnp.sqrt(power) + water_level * spread)
    for part, value in enumerate((real * factor, imag * factor)):
        for w in range(WIN):
            for high in range(2):
                x = value[w * OWN : (w + 1) * OWN, high * 128 : (high + 1) * 128]
                for bit in range(3):
                    x = swap_bits(x, 2**bit, 16 * 2**bit)
                line_ref[pl.ds(32 * high + 2 * w + part, 8, stride=4), :] = x
    out_ref[...] = line_ref[...].astype(BF16)


def turn_kernel(in_ref, out_ref):
    x = in_ref[...].astype(F32)
    for bit in range(4):
        x = swap_bits(x, 4 * 2**bit, 2**bit)
    x = x.astype(BF16)
    out_ref[:64, :] = x
    out_ref[64:, :] = x


def coherence_kernel(half_ref, one_hot_ref, perm_ref, in_ref, out_any, all_ref, out_ref, sems):
    x = in_ref[...].astype(F32)

    def piece(w, c, y):
        start = ((w * 2 + c) * 4 + y) * 8
        return x[start : start + 8]

    stacked = jnp.concatenate(
        [
            jnp.concatenate([piece(w, c, y) for y in range(4) for w in range(2)], axis=0)
            for c in range(2)
        ],
        axis=1,
    ).astype(BF16)
    ordered = jnp.dot(stacked, perm_ref[...], preferred_element_type=F32)
    every = jnp.concatenate([ordered[16 * y : 16 * (y + 1)] for y in range(4)], axis=1)
    all_ref[...] = every
    half = half_ref[0]
    receivers = all_ref[:, pl.ds(pl.multiple_of(half * 512, 512), 512)]
    chosen = jnp.dot(every.astype(BF16), one_hot_ref[...], preferred_element_type=F32)
    even = iota(receivers.shape, 0) % 2 == 0
    turned = jnp.where(even, pltpu.roll(receivers, 15, 0), -pltpu.roll(receivers, 1, 0))
    chosen_t = chosen.T
    energy_src = jnp.sum(chosen_t * chosen_t, axis=1, keepdims=True)
    energy_rec = jnp.sum(receivers * receivers, axis=0, keepdims=True)
    scale = lax.rsqrt(jnp.maximum(energy_src * energy_rec, 1.0))
    left = chosen_t.astype(BF16)
    copies = []
    for part, right in enumerate((receivers, turned)):
        out_ref[part] = jnp.dot(left, right.astype(BF16), preferred_element_type=F32) * scale
        copies.append(pltpu.make_async_copy(out_ref.at[part], out_any.at[0, part], sems.at[part]))
        copies[-1].start()
    for copy in copies:
        copy.wait()


VMEM = pl.BlockSpec(memory_space=pltpu.VMEM)
SMEM = pl.BlockSpec(memory_space=pltpu.SMEM)
PARAMS = pltpu.CompilerParams(vmem_limit_bytes=32 * 1024 * 1024)


def prepare(conv_weight, in_weight, out_weight, sources, raw, flags):
    arrays = (
        conv_weight.transpose(0, 3, 4, 1, 2), in_weight.T, out_weight.reshape(1, F), sources.reshape(1, NV),
        raw, flags, jnp.asarray(sample_perm()), jnp.asarray(dft_table()), jnp.asarray(channel_perm()),
    )
    arrays = tuple(pltpu.with_memory_space_constraint(a, pltpu.HBM) for a in arrays)
    return pl.pallas_call(
        prepare_kernel,
        out_shape=(
            jax.ShapeDtypeStruct((LAYERS, BLK * F, 3 * 256), BF16),
            jax.ShapeDtypeStruct((EXT * F, 72), BF16),
            jax.ShapeDtypeStruct((OWN, OWN * F), BF16),
            jax.ShapeDtypeStruct((CH_ALL, NV), BF16),
        )
        + tuple(jax.ShapeDtypeStruct(a.shape, a.dtype) for a in arrays[4:]),
        in_specs=[pl.BlockSpec(memory_space=pl.ANY)] * 9,
        out_specs=(VMEM,) * 9,
        scratch_shapes=[pltpu.VMEM(a.shape, a.dtype) for a in arrays[:4]]
        + [pltpu.SemaphoreType.DMA((9,))],
        compiler_params=PARAMS,
        cost_estimate=pl.CostEstimate(flops=2_000_000, bytes_accessed=4_000_000, transcendentals=0),
        name="prepare",
    )(*arrays)


def denoise(edge, near, raw, far, flags, order, band, first, last, table):
    return pl.pallas_call(
        denoise_kernel,
        out_shape=jax.ShapeDtypeStruct((64, 128), BF16),
        in_specs=[SMEM] + [VMEM] * 9,
        out_specs=VMEM,
        scratch_shapes=[pltpu.VMEM(((EXT - 2 * i) * F, WIDE), BF16) for i in range(LAYERS + 1)]
        + [pltpu.VMEM((EXT * F, WIDE), BF16)] * 2
        + [pltpu.VMEM((64, 128), F32)],
        compiler_params=PARAMS,
        name="denoise",
    )(edge, near, raw, far, flags, order, band, first, last, table)


def turn(rows):
    return pl.pallas_call(
        turn_kernel,
        out_shape=jax.ShapeDtypeStruct((128, 128), BF16),
        in_specs=[VMEM],
        out_specs=VMEM,
        compiler_params=PARAMS,
        name="turn",
    )(rows)


def coherence(half, one_hot, perm, rows):
    return pl.pallas_call(
        coherence_kernel,
        out_shape=jax.ShapeDtypeStruct((1, 2, 128, 512), F32),
        in_specs=[SMEM, VMEM, VMEM, VMEM],
        out_specs=pl.BlockSpec(memory_space=pl.ANY),
        scratch_shapes=[
            pltpu.VMEM((16, CH_ALL), F32),
            pltpu.VMEM((2, 128, 512), F32),
            pltpu.SemaphoreType.DMA((2,)),
        ],
        compiler_params=PARAMS,
        name="coherence",
    )(half, one_hot, perm, rows)


CHAN = ("y", "z", "c")


def per_device(raw, flags, in_weight, conv_weight, out_weight, sources):
    count = lax.axis_size(CHAN)
    me = lax.axis_index(CHAN)
    odd = lax.axis_index("c")
    across = [(i, i + 1) for i in range(1, count - 1, 2)]
    far = lax.ppermute(raw, CHAN, across + [(b, a) for a, b in across])
    near = lax.ppermute(raw, "c", [(0, 1), (1, 0)])
    edge = jnp.stack([me == 0, me == count - 1, odd == 1]).astype(jnp.int32)
    half = lax.axis_index("w").reshape(1).astype(jnp.int32)
    band, first, last, one_hot, raw, flags, order, table, perm = prepare(
        conv_weight, in_weight, out_weight, sources, raw, flags
    )
    sent = denoise(edge, near, raw, far, flags, order, band, first, last, table)
    half, sent = lax.optimization_barrier((half, sent))
    got = lax.all_to_all(sent, "z", 0, 0, tiled=True)
    mine = lax.all_to_all(turn(got), ("w", "c", "y", "s"), 0, 0, tiled=True)
    return coherence(half, one_hot, perm, mine)


def solution(mesh):
    fine = Mesh(mesh.devices.reshape(2, 4, 16, 2, 2), ("s", "y", "z", "c", "w"))
    placed = (P(("s", "w"), CHAN, None), P(("s", "w"), CHAN), P(), P(), P(), P())
    return jax.shard_map(
        per_device,
        mesh=fine,
        in_specs=placed,
        out_specs=P(("s",) + CHAN, None, None, "w"),
        check_vma=False,
    )
```

time: 59.8 us -> 57.7 us (0.965)
  Pallas kernels: 9.32 us -> 7.46 us
    pallas_call x1, Pallas kernels: 6.28 us -> 4.2 us  [denoise(): pl.pallas_call(denoise_kernel, out_shape=jax.ShapeDtypeStruct((64, 128),...]
  transfers between devices with their start and end apart: 2 -> 2, of which waited for: 1 -> 1; matrix products, arithmetic and copies ran while one was open for 0% -> 0% of each run, Pallas kernels for 2% -> 3%
where the time goes in v2:
time: 57.7 us; the launch traced here: 57.4 us
  blocking collectives  37.5 us (65%)
  starting transfers between devices  10.7 us (19%)
  Pallas kernels  7.46 us (13%)
  waiting for transfers between devices  1.66 us (3%)
    all_to_all x1, blocking collectives, per_device(): got = lax.all_to_all(sent, 'z', 0, 0, tiled=True)  21 us
    all_to_all x1, blocking collectives, per_device(): mine = lax.all_to_all(turn(got), ('w', 'c', 'y', 's'), 0, 0, tiled=True)  16.5 us
    ppermute x1, starting transfers between devices, per_device(): near = lax.ppermute(raw, 'c', [(0, 1), (1, 0)])  8.78 us
    pallas_call x1, Pallas kernels, denoise(): pl.pallas_call(denoise_kernel, out_shape=jax.ShapeDtypeStruct((64, 128),...  4.2 us
    ppermute x1, starting transfers between devices, per_device(): far = lax.ppermute(raw, CHAN, across + [(b, a) for a, b in across])  1.92 us
    ppermute x1, waiting for transfers between devices, per_device(): far = lax.ppermute(raw, CHAN, across + [(b, a) for a, b in across])  1.65 us
    pallas_call x1, Pallas kernels, prepare(): pl.pallas_call(prepare_kernel, out_shape=(jax.ShapeDtypeStruct((LAYERS, B...  1.62 us
    pallas_call x1, Pallas kernels, coherence(): pl.pallas_call(coherence_kernel, out_shape=jax.ShapeDtypeStruct((1, 2, 12...  1.34 us
  transfers between devices with their start and end apart: 2, of which 1 were waited for; matrix products, arithmetic and copies ran while one was open for 0% of the time, Pallas kernels for 3%

profile of v2, /device:TPU:1, one launch (start us, length us, event | category | flops | bytes accessed | tf_op | source)
XLA Modules:
  0.0 57.4 jit_solution(6488832092779205601)
XLA Ops:
  0.0 8.8 %collective-permute-start = (bf16[2,8,640]{2,1,0:T(8,128)(2,1)}, bf16[2,8,640]{2,1,0:T(8,128)(2,1)S(1)}, u32[]{:S(2)}, u32[]{:S(2)}) collective-permute-start(bf16[2,8,640]{2,1,0:T(8,128)(2,1)} %raw_any.1), channel_id=1, source_target_pairs={{0,2},{2,0},{1,3},{3,1},{4,6},{6,4},{5,7},{7,5},{8,10},{10,8},{9,1... | collective-permute-start | bytes 61448 | tf_op jit(solution)/shard_map/ppermute | solution.py:340
  8.8 1.9 %collective-permute-start.1 = (bf16[2,8,640]{2,1,0:T(8,128)(2,1)}, bf16[2,8,640]{2,1,0:T(8,128)(2,1)S(1)}, u32[]{:S(2)}, u32[]{:S(2)}) collective-permute-start(bf16[2,8,640]{2,1,0:T(8,128)(2,1)} %raw_any.1), channel_id=1, source_target_pairs={{2,4},{6,8},{10,12},{14,16},{18,20},{22,24},{26,28},{30,32},{34,36... | collective-permute-start | bytes 61448 | tf_op jit(solution)/shard_map/ppermute | solution.py:339
  10.7 0.1 add_convert_fusion.edge_ref
  10.8 1.6 %prepare.1 = (bf16[3,192,768]{2,1,0:T(8,128)(2,1)S(1)}, bf16[448,72]{1,0:T(8,128)(2,1)S(1)}, bf16[8,256]{1,0:T(8,128)(2,1)S(1)}, bf16[1024,128]{1,0:T(8,128)(2,1...) custom-call(bf16[3,3,3,32,32]{4,3,2,1,0:T(8,128)(2,1)} %bitcast.16, ...), custom_call_target="tpu_custom_call" | custom-call | flops 2000000 | bytes 4000000 | tf_op jit(solution)/shard_map/prepare/pallas_call | solution.py:271
  12.4 0.0 collective-permute-done.near_ref
  12.4 1.7 %collective-permute-done.1.far_ref = bf16[2,8,640]{2,1,0:T(8,128)(2,1)S(1)} collective-permute-done((bf16[2,8,640]{2,1,0:T(8,128)(2,1)}, bf16[2,8,640]{2,1,0:T(8,128)(2,1)S(1)}, u32[]{:S(2)}, u32[]{:S(2)}) %collective-permute-start.1) | collective-permute-done | bytes 20512 | tf_op jit(solution)/shard_map/ppermute | solution.py:339
  14.1 4.2 %denoise.1 = bf16[64,128]{1,0:T(8,128)(2,1)S(1)} custom-call(s32[3]{0:T(128)S(1)} %add_convert_fusion.edge_ref, bf16[2,8,640]{2,1,0:T(8,128)(2,1)S(1)} %collective-permute-done.near_ref, bf16[2,8,640]{2,1,0:T(8,128)(2,1)S(1)} %get-tuple-element.16.raw_ref, bf16[2,8,640]{2,1,0:T(8,128)(2,1)S(1)} %collective-permute-done.1.far_ref, ...), custom_call_target="tpu_custom_call" | custom-call | tf_op jit(solution)/shard_map/denoise/pallas_call | solution.py:291
  18.3 21.0 %all_to_all.22 = bf16[16,4,128]{2,1,0:T(4,128)(2,1)S(1)} all-to-all(bf16[16,4,128]{2,1,0:T(4,128)(2,1)S(1)} %bitcast.15), channel_id=1, replica_groups=mesh['s'=2,'y'=4,'z'=16,'c'=2,'w'=2] {'z'}, dimensions={0} | all-to-all | bytes 32768 | tf_op jit(solution)/shard_map/all_to_all | solution.py:348
  39.3 0.3 turn.1
  39.6 16.5 %all_to_all.23 = bf16[32,4,128]{2,1,0:T(4,128)(2,1)S(1)} all-to-all(bf16[32,4,128]{2,1,0:T(4,128)(2,1)S(1)} %bitcast.13), channel_id=1, replica_groups=mesh['s'=2,'y'=4,'z'=16,'c'=2,'w'=2] {'w','c','y','s'}, dimensions={0} | all-to-all | bytes 65536 | tf_op jit(solution)/shard_map/all_to_all | solution.py:349
  56.1 1.3 %coherence.1 = f32[1,2,128,512]{3,2,1,0:T(8,128)} custom-call(s32[1]{0:T(128)} %bitcast.half_ref, bf16[1024,128]{1,0:T(8,128)(2,1)S(1)} %get-tuple-element.24.one_hot_ref, bf16[256,256]{1,0:T(8,128)(2,1)S(1)} %get-tuple-element.25.perm_ref, bf16[128,128]{1,0:T(8,128)(2,1)S(1)} %bitcast.12), custom_call_target="tpu_custom_call" | custom-call | tf_op jit(solution)/shard_map/coherence/pallas_call | solution.py:316
Async XLA Ops:
  0.0 12.4 %collective-permute-start = (bf16[2,8,640]{2,1,0:T(8,128)(2,1)}, bf16[2,8,640]{2,1,0:T(8,128)(2,1)S(1)}, u32[]{:S(2)}, u32[]{:S(2)}) collective-permute-start(bf16[2,8,640]{2,1,0:T(8,128)(2,1)} %raw_any.1), channel_id=1, source_target_pairs={{0,2},{2,0},{1,3},{3,1},{4,6},{6,4},{5,7},{7,5},{8,10},{10,8},{9,1... | collective-permute-start | bytes 61448 | tf_op jit(solution)/shard_map/ppermute | solution.py:340
  8.8 5.3 %collective-permute-start.1 = (bf16[2,8,640]{2,1,0:T(8,128)(2,1)}, bf16[2,8,640]{2,1,0:T(8,128)(2,1)S(1)}, u32[]{:S(2)}, u32[]{:S(2)}) collective-permute-start(bf16[2,8,640]{2,1,0:T(8,128)(2,1)} %raw_any.1), channel_id=1, source_target_pairs={{2,4},{6,8},{10,12},{14,16},{18,20},{22,24},{26,28},{30,32},{34,36... | collective-permute-start | bytes 61448 | tf_op jit(solution)/shard_map/ppermute | solution.py:339

commit v3 on v2

--- a/solution.py
+++ b/solution.py
@@ -23,6 +23,9 @@
 WIDE = WIN * NT
 CH_ALL = 1024
 NV = 128
+Y_ORDER = (2, 3, 0, 1)
+W_ORDER = (1, 0)
+Z_ORDER = tuple((np.arange(16) + 8) % 16)
 
 water_level = 0.2
 epsilon_power = 1e-06
@@ -33,7 +36,7 @@
 
 def dft_table():
     part, z, core, y, section = np.meshgrid(
-        np.arange(2), np.arange(16), np.arange(2), np.arange(4), np.arange(2), indexing="ij"
+        np.arange(2), np.array(Z_ORDER), np.arange(2), np.array(Y_ORDER), np.arange(2), indexing="ij"
     )
     k = (section * 128 + (y * 16 + z) * 2 + core).reshape(-1)
     part = part.reshape(-1)
@@ -52,7 +55,7 @@
 
 
 def channel_perm():
-    core, channel, z = np.meshgrid(np.arange(2), np.arange(OWN), np.arange(16), indexing="ij")
+    core, channel, z = np.meshgrid(np.arange(2), np.arange(OWN), np.array(Z_ORDER), indexing="ij")
     target = ((z * 2 + core) * OWN + channel).reshape(-1)
     return np.eye(256, dtype=np.float32)[target].astype(BF16)
 
@@ -132,7 +135,7 @@
 
 
 def denoise_kernel(
-    edge_ref, near_ref, raw_ref, far_ref, flags_ref, order_ref, band_ref, first_ref, last_ref, table_ref,
+    edge_ref, far_ref, raw_ref, near_ref, flags_ref, order_ref, band_ref, first_ref, last_ref, table_ref,
     out_ref, h0_ref, h1_ref, h2_ref, h3_ref, earlier_ref, later_ref, line_ref,
 ):
     is_first, is_last, odd = edge_ref[0], edge_ref[1], edge_ref[2]
@@ -225,7 +228,7 @@
     x = in_ref[...].astype(F32)
 
     def piece(w, c, y):
-        start = ((w * 2 + c) * 4 + y) * 8
+        start = ((w * 2 + c) * 4 + Y_ORDER.index(y)) * 8
         return x[start : start + 8]
 
     stacked = jnp.concatenate(
@@ -287,7 +290,7 @@
     )(*arrays)
 
 
-def denoise(edge, near, raw, far, flags, order, band, first, last, table):
+def denoise(edge, far, raw, near, flags, order, band, first, last, table):
     return pl.pallas_call(
         denoise_kernel,
         out_shape=jax.ShapeDtypeStruct((64, 128), BF16),
@@ -298,7 +301,7 @@
         + [pltpu.VMEM((64, 128), F32)],
         compiler_params=PARAMS,
         name="denoise",
-    )(edge, near, raw, far, flags, order, band, first, last, table)
+    )(edge, far, raw, near, flags, order, band, first, last, table)
 
 
 def turn(rows):
@@ -336,17 +339,20 @@
     me = lax.axis_index(CHAN)
     odd = lax.axis_index("c")
     across = [(i, i + 1) for i in range(1, count - 1, 2)]
+    near = lax.ppermute(raw, "c", [(0, 1), (1, 0)])
     far = lax.ppermute(raw, CHAN, across + [(b, a) for a, b in across])
-    near = lax.ppermute(raw, "c", [(0, 1), (1, 0)])
     edge = jnp.stack([me == 0, me == count - 1, odd == 1]).astype(jnp.int32)
     half = lax.axis_index("w").reshape(1).astype(jnp.int32)
     band, first, last, one_hot, raw, flags, order, table, perm = prepare(
         conv_weight, in_weight, out_weight, sources, raw, flags
     )
-    sent = denoise(edge, near, raw, far, flags, order, band, first, last, table)
+    sent = denoise(edge, far, raw, near, flags, order, band, first, last, table)
     half, sent = lax.optimization_barrier((half, sent))
-    got = lax.all_to_all(sent, "z", 0, 0, tiled=True)
-    mine = lax.all_to_all(turn(got), ("w", "c", "y", "s"), 0, 0, tiled=True)
+    got = lax.all_to_all(
+        sent, "z", 0, 0, tiled=True, axis_index_groups=[[int(z) for z in Z_ORDER]]
+    )
+    rest = [((w * 2 + c) * 4 + y) * 2 + s for w in W_ORDER for c in range(2) for y in Y_ORDER for s in range(2)]
+    mine = lax.all_to_all(turn(got), ("w", "c", "y", "s"), 0, 0, tiled=True, axis_index_groups=[rest])
     return coherence(half, one_hot, perm, mine)
 
 

time: 57.7 us -> 47.5 us (0.82)
  blocking collectives: 37.5 us -> 30.2 us
  waiting for transfers between devices: 1.66 us -> 0.01 us
  starting transfers between devices: 10.7 us -> 9.44 us
    all_to_all x2, blocking collectives: 37.5 us -> 30.2 us  [the longest x1 17.4 us: per_device(): lax.all_to_all(sent, 'z', 0, 0, tiled=True, axis_index_groups=[[int(z) fo...]
    ppermute x1, starting transfers between devices: 8.78 us -> 4.51 us  [per_device(): near = lax.ppermute(raw, 'c', [(0, 1), (1, 0)])]
    ppermute x1, starting transfers between devices: 1.92 us -> 4.93 us  [per_device(): far = lax.ppermute(raw, CHAN, across + [(b, a) for a, b in across])]
    ppermute x1, waiting for transfers between devices: 1.65 us -> 0.01 us  [per_device(): far = lax.ppermute(raw, CHAN, across + [(b, a) for a, b in across])]
  transfers between devices with their start and end apart: 2 -> 2, of which waited for: 1 -> 0; matrix products, arithmetic and copies ran while one was open for 0% -> 0% of each run, Pallas kernels for 3% -> 3%
where the time goes in v3:
time: 47.5 us; the launch traced here: 47.2 us
  blocking collectives  30.2 us (64%)
  starting transfers between devices  9.44 us (20%)
  Pallas kernels  7.47 us (16%)
    all_to_all x1, blocking collectives, per_device(): lax.all_to_all(sent, 'z', 0, 0, tiled=True, axis_index_groups=[[int(z) fo...  17.4 us
    all_to_all x1, blocking collectives, per_device(): lax.all_to_all(turn(got), ('w', 'c', 'y', 's'), 0, 0, tiled=True, axis_in...  12.8 us
    ppermute x1, starting transfers between devices, per_device(): far = lax.ppermute(raw, CHAN, across + [(b, a) for a, b in across])  4.93 us
    ppermute x1, starting transfers between devices, per_device(): near = lax.ppermute(raw, 'c', [(0, 1), (1, 0)])  4.51 us
    pallas_call x1, Pallas kernels, denoise(): pl.pallas_call(denoise_kernel, out_shape=jax.ShapeDtypeStruct((64, 128),...  4.21 us
    pallas_call x1, Pallas kernels, prepare(): pl.pallas_call(prepare_kernel, out_shape=(jax.ShapeDtypeStruct((LAYERS, B...  1.62 us
    pallas_call x1, Pallas kernels, coherence(): pl.pallas_call(coherence_kernel, out_shape=jax.ShapeDtypeStruct((1, 2, 12...  1.34 us
  transfers between devices with their start and end apart: 2, of which 0 were waited for; matrix products, arithmetic and copies ran while one was open for 0% of the time, Pallas kernels for 3%

profile of v3, /device:TPU:1, one launch (start us, length us, event | category | flops | bytes accessed | tf_op | source)
XLA Modules:
  0.0 47.2 jit_solution(16614393986281303362)
XLA Ops:
  0.0 4.9 %collective-permute-start = (bf16[2,8,640]{2,1,0:T(8,128)(2,1)}, bf16[2,8,640]{2,1,0:T(8,128)(2,1)S(1)}, u32[]{:S(2)}, u32[]{:S(2)}) collective-permute-start(bf16[2,8,640]{2,1,0:T(8,128)(2,1)} %raw_any.1), channel_id=1, source_target_pairs={{2,4},{6,8},{10,12},{14,16},{18,20},{22,24},{26,28},{30,32},{34,36... | collective-permute-start | bytes 61448 | tf_op jit(solution)/shard_map/ppermute | solution.py:343
  4.9 4.5 %collective-permute-start.1 = (bf16[2,8,640]{2,1,0:T(8,128)(2,1)}, bf16[2,8,640]{2,1,0:T(8,128)(2,1)S(1)}, u32[]{:S(2)}, u32[]{:S(2)}) collective-permute-start(bf16[2,8,640]{2,1,0:T(8,128)(2,1)} %raw_any.1), channel_id=1, source_target_pairs={{0,2},{2,0},{1,3},{3,1},{4,6},{6,4},{5,7},{7,5},{8,10},{10,8},{9,1... | collective-permute-start | bytes 61448 | tf_op jit(solution)/shard_map/ppermute | solution.py:342
  9.5 0.1 add_convert_fusion.edge_ref
  9.5 1.6 %prepare.1 = (bf16[3,192,768]{2,1,0:T(8,128)(2,1)S(1)}, bf16[448,72]{1,0:T(8,128)(2,1)S(1)}, bf16[8,256]{1,0:T(8,128)(2,1)S(1)}, bf16[1024,128]{1,0:T(8,128)(2,1...) custom-call(bf16[3,3,3,32,32]{4,3,2,1,0:T(8,128)(2,1)} %bitcast.16, ...), custom_call_target="tpu_custom_call" | custom-call | flops 2000000 | bytes 4000000 | tf_op jit(solution)/shard_map/prepare/pallas_call | solution.py:274
  11.2 0.0 collective-permute-done.far_ref
  11.2 0.0 collective-permute-done.1.near_ref
  11.2 4.2 %denoise.1 = bf16[64,128]{1,0:T(8,128)(2,1)S(1)} custom-call(s32[3]{0:T(128)S(1)} %add_convert_fusion.edge_ref, bf16[2,8,640]{2,1,0:T(8,128)(2,1)S(1)} %collective-permute-done.far_ref, bf16[2,8,640]{2,1,0:T(8,128)(2,1)S(1)} %get-tuple-element.16.raw_ref, bf16[2,8,640]{2,1,0:T(8,128)(2,1)S(1)} %collective-permute-done.1.near_ref, ...), custom_call_target="tpu_custom_call" | custom-call | tf_op jit(solution)/shard_map/denoise/pallas_call | solution.py:294
  15.4 17.4 %all_to_all.22 = bf16[16,4,128]{2,1,0:T(4,128)(2,1)S(1)} all-to-all(bf16[16,4,128]{2,1,0:T(4,128)(2,1)S(1)} %bitcast.15), channel_id=1, replica_groups={{32,36,40,44,48,52,56,60,0,4,8,12,16,20,24,28},{33,37,41,45,49,53,57,61..., dimensions={0} | all-to-all | bytes 32768 | tf_op jit(solution)/shard_map/all_to_all | solution.py:351
  32.8 0.3 turn.1
  33.1 12.8 %all_to_all.23 = bf16[32,4,128]{2,1,0:T(4,128)(2,1)S(1)} all-to-all(bf16[32,4,128]{2,1,0:T(4,128)(2,1)S(1)} %bitcast.13), channel_id=1, replica_groups={{129,385,193,449,1,257,65,321,131,387,195,451,3,259,67,323,128,384,192,..., dimensions={0} | all-to-all | bytes 65536 | tf_op jit(solution)/shard_map/all_to_all | solution.py:355
  45.9 1.3 %coherence.1 = f32[1,2,128,512]{3,2,1,0:T(8,128)} custom-call(s32[1]{0:T(128)} %bitcast.half_ref, bf16[1024,128]{1,0:T(8,128)(2,1)S(1)} %get-tuple-element.24.one_hot_ref, bf16[256,256]{1,0:T(8,128)(2,1)S(1)} %get-tuple-element.25.perm_ref, bf16[128,128]{1,0:T(8,128)(2,1)S(1)} %bitcast.12), custom_call_target="tpu_custom_call" | custom-call | tf_op jit(solution)/shard_map/coherence/pallas_call | solution.py:319
Async XLA Ops:
  0.0 11.2 %collective-permute-start = (bf16[2,8,640]{2,1,0:T(8,128)(2,1)}, bf16[2,8,640]{2,1,0:T(8,128)(2,1)S(1)}, u32[]{:S(2)}, u32[]{:S(2)}) collective-permute-start(bf16[2,8,640]{2,1,0:T(8,128)(2,1)} %raw_any.1), channel_id=1, source_target_pairs={{2,4},{6,8},{10,12},{14,16},{18,20},{22,24},{26,28},{30,32},{34,36... | collective-permute-start | bytes 61448 | tf_op jit(solution)/shard_map/ppermute | solution.py:343
  4.9 6.3 %collective-permute-start.1 = (bf16[2,8,640]{2,1,0:T(8,128)(2,1)}, bf16[2,8,640]{2,1,0:T(8,128)(2,1)S(1)}, u32[]{:S(2)}, u32[]{:S(2)}) collective-permute-start(bf16[2,8,640]{2,1,0:T(8,128)(2,1)} %raw_any.1), channel_id=1, source_target_pairs={{0,2},{2,0},{1,3},{3,1},{4,6},{6,4},{5,7},{7,5},{8,10},{10,8},{9,1... | collective-permute-start | bytes 61448 | tf_op jit(solution)/shard_map/ppermute | solution.py:342

commit v4 on v3

--- a/solution.py
+++ b/solution.py
@@ -78,29 +78,42 @@
     return jnp.where(row_bit == lane_bit, x, jnp.where(row_bit == 0, down, up))
 
 
+def pack_kernel(raw_any, flags_any, own_ref, flags_ref, sems):
+    copies = (
+        pltpu.make_async_copy(flags_any, flags_ref, sems.at[0]),
+        pltpu.make_async_copy(raw_any, own_ref.at[:, :, pl.ds(0, NT)], sems.at[1]),
+    )
+    for copy in copies:
+        copy.start()
+    copies[0].wait()
+    for w in range(WIN):
+        flags = column(flags_ref[w : w + 1, :].astype(F32), OWN)
+        own_ref[w, :, NT:] = jnp.broadcast_to(flags, (OWN, LANES)).astype(BF16)
+    copies[1].wait()
+
+
 def prepare_kernel(
-    conv_any, in_any, out_any, sources_any, raw_any, flags_any, order_any, table_any, perm_any,
-    band_ref, first_ref, last_ref, one_hot_ref, raw_ref, flags_ref, order_ref, table_ref, perm_ref,
+    cut_ref, conv_any, in_any, out_any, sources_any, order_any, table_any, perm_any,
+    band_ref, first_ref, last_ref, one_hot_ref, order_ref, table_ref, perm_ref,
     conv_ref, in_ref, out_ref, sources_ref, sems,
 ):
     pairs = (
         (conv_any, conv_ref), (in_any, in_ref), (out_any, out_ref), (sources_any, sources_ref),
-        (raw_any, raw_ref), (flags_any, flags_ref), (order_any, order_ref), (table_any, table_ref),
-        (perm_any, perm_ref),
+        (order_any, order_ref), (table_any, table_ref), (perm_any, perm_ref),
     )
     copies = [pltpu.make_async_copy(a, b, sems.at[i]) for i, (a, b) in enumerate(pairs)]
     for copy in copies:
         copy.start()
     copies[1].wait()
-    shape = (EXT * F, 72)
+    shape = (EXT * F, 48)
     channel = iota(shape, 0) // F
-    place = jnp.where(channel < 3, 13 + channel, jnp.where(channel < 11, channel - 3, channel + 5))
+    place = jnp.where(channel < 7, OWN + 1 + channel, channel - 7)
     lane = iota(shape, 1)
     first = jnp.zeros(shape, F32)
     for tap in range(3):
         weight = column(in_ref[tap : tap + 1, :].astype(F32), F)
         tall = jnp.broadcast_to(jnp.concatenate([weight] * EXT, axis=0), shape)
-        first = jnp.where(lane == place + 24 * tap, tall, first)
+        first = jnp.where(lane == place + 16 * tap, tall, first)
     first_ref[...] = first.astype(BF16)
     copies[2].wait()
     shape = (OWN, OWN * F)
@@ -110,9 +123,10 @@
     ).astype(BF16)
     copies[3].wait()
     shape = (CH_ALL, NV)
-    one_hot_ref[...] = jnp.where(
-        iota(shape, 0) == jnp.broadcast_to(sources_ref[...], shape), 1.0, 0.0
-    ).astype(BF16)
+    j = (sources_ref[...] + OWN // 2) % CH_ALL
+    z = ((j // 16) % 16 - Z_ORDER[0]) % 16
+    row = (j // 256) * 256 + ((j // 8) % 2) * 128 + (j % 8) * 16 + z
+    one_hot_ref[...] = jnp.where(iota(shape, 0) == jnp.broadcast_to(row, shape), 1.0, 0.0).astype(BF16)
     copies[0].wait()
     for layer in range(LAYERS):
         for tap in range(3):
@@ -120,7 +134,20 @@
             base = jnp.concatenate(taps + [jnp.zeros((F, 256 - 3 * F), BF16)], axis=1)
             for c in range(BLK):
                 row = base if c == 0 else pltpu.roll(base, F * c, 1)
-                band_ref[layer, F * c : F * (c + 1), 256 * tap : 256 * (tap + 1)] = row
+                for block in range(2):
+                    band_ref[layer, block, F * c : F * (c + 1), 256 * tap : 256 * (tap + 1)] = row
+
+    @pl.when(cut_ref[0] == 1)
+    def _():
+        for layer in range(LAYERS):
+            for block in range(2):
+                start = block * (EXT - 2 * (layer + 1) - BLK) + layer
+                for c, k in ((5 - start, 7 - start), (6 - start, 6 - start)):
+                    if 0 <= c < BLK:
+                        for tap in range(3):
+                            lanes = slice(256 * tap + F * k, 256 * tap + F * (k + 1))
+                            band_ref[layer, block, F * c : F * (c + 1), lanes] = jnp.zeros((F, F), BF16)
+
     for copy in copies[4:]:
         copy.wait()
 
@@ -135,18 +162,15 @@
 
 
 def denoise_kernel(
-    edge_ref, far_ref, raw_ref, near_ref, flags_ref, order_ref, band_ref, first_ref, last_ref, table_ref,
+    own_ref, left_ref, order_ref, band_ref, first_ref, last_ref, table_ref,
     out_ref, h0_ref, h1_ref, h2_ref, h3_ref, earlier_ref, later_ref, line_ref,
 ):
-    is_first, is_last, odd = edge_ref[0], edge_ref[1], edge_ref[2]
-    near, far = near_ref[...].astype(F32), far_ref[...].astype(F32)
-    left, right = jnp.where(odd == 1, near, far), jnp.where(odd == 1, far, near)
-    rows = [x for w in range(WIN) for x in (raw_ref[w].astype(F32), left[w], right[w])]
+    rows = [ref[w, :, :NT].astype(F32) for w in range(WIN) for ref in (own_ref, left_ref)]
     rows = jnp.concatenate(rows, axis=0).astype(BF16)
     rows = jnp.dot(rows, order_ref[...], preferred_element_type=F32)
     lines = [
         jnp.concatenate(
-            [rows[24 * w : 24 * (w + 1), v * LANES : (v + 1) * LANES] for w in range(WIN)], axis=1
+            [rows[16 * w : 16 * (w + 1), v * LANES : (v + 1) * LANES] for w in range(WIN)], axis=1
         )
         for v in range(PH)
     ]
@@ -157,12 +181,12 @@
         after = lines[v + 1] if v < PH - 1 else lane_shift(lines[0], -1)
         taps = jnp.concatenate([before, lines[v], after], axis=0).astype(BF16)
         h0_ref[:, chunk[v]] = jnp.dot(first_ref[...], taps, preferred_element_type=F32).astype(BF16)
+    spectra = None
     for layer in range(LAYERS):
         step = 2**layer
         source, target = hidden[layer], hidden[layer + 1]
         size = (EXT - 2 * layer) * F
         count = EXT - 2 * (layer + 1)
-        reach = LAYERS - 1 - layer
         for v in sorted(range(PH), key=lambda v: (v < step) + (v >= PH - step)):
             before, after, u, t = source, source, v - step, v + step
             if u < 0:
@@ -173,36 +197,28 @@
                 t -= PH
                 after = later_ref
                 later_ref[:size, chunk[t]] = lane_shift(source[:, chunk[t]], -1)
-            for start, low in ((0, 0), (count - BLK, 2 * BLK - count)):
+            for block, start, low in ((0, 0, 0), (1, count - BLK, 2 * BLK - count)):
                 k = slice(start * F, (start + BLK + 2) * F)
                 taps = jnp.concatenate([before[k, chunk[u]], source[k, chunk[v]], after[k, chunk[t]]], axis=0)
-                total = jnp.dot(band_ref[layer, low * F :, :], taps, preferred_element_type=F32)
+                total = jnp.dot(band_ref[layer, block, low * F :, :], taps, preferred_element_type=F32)
                 old = source[(start + low + 1) * F : (start + BLK + 1) * F, chunk[v]].astype(F32)
                 new = old + jnp.maximum(total, 0.0)
-                for i in range(BLK - low):
-                    c = start + low + i
-                    part = new[i * F : (i + 1) * F]
-                    if c < reach:
-                        part = jnp.where(is_first == 1, 0.0, part)
-                    if c >= count - reach:
-                        part = jnp.where(is_last == 1, 0.0, part)
-                    target[c * F : (c + 1) * F, chunk[v]] = part.astype(BF16)
-    clean = jnp.dot(last_ref[...], h3_ref[...], preferred_element_type=F32)
-    clean = jnp.concatenate(
-        [
-            jnp.concatenate(
-                [clean[:, v * CHUNK + w * LANES : v * CHUNK + (w + 1) * LANES] for v in range(PH)], axis=1
-            )
-            for w in range(WIN)
-        ],
-        axis=0,
-    )
-    spectra = jnp.dot(clean.astype(BF16), table_ref[...], preferred_element_type=F32)
+                target[(start + low) * F : (start + BLK) * F, chunk[v]] = new.astype(BF16)
+            if layer == LAYERS - 1:
+                clean = jnp.dot(last_ref[...], target[:, chunk[v]], preferred_element_type=F32)
+                clean = jnp.concatenate([clean[:, :LANES], clean[:, LANES:]], axis=0).astype(BF16)
+                term = jnp.dot(clean, table_ref[v * LANES : (v + 1) * LANES, :], preferred_element_type=F32)
+                spectra = term if spectra is None else spectra + term
     real, imag = spectra[:, :NF], spectra[:, NF:]
     power = real * real + imag * imag
     spread = jnp.sqrt(jnp.mean(power, axis=1, keepdims=True) + epsilon_power)
     flags = jnp.concatenate(
-        [column(flags_ref[w : w + 1, :].astype(F32), OWN) for w in range(WIN)], axis=0
+        [
+            ref[w, :, NT : NT + 1].astype(F32)[part]
+            for w in range(WIN)
+            for ref, part in ((left_ref, slice(4, 8)), (own_ref, slice(0, 4)))
+        ],
+        axis=0,
     )
     factor = flags / (jnp.sqrt(power) + water_level * spread)
     for part, value in enumerate((real * factor, imag * factor)):
@@ -240,10 +256,11 @@
     ).astype(BF16)
     ordered = jnp.dot(stacked, perm_ref[...], preferred_element_type=F32)
     every = jnp.concatenate([ordered[16 * y : 16 * (y + 1)] for y in range(4)], axis=1)
-    all_ref[...] = every
+    all_ref[...] = pltpu.roll(every, CH_ALL - OWN // 2, 1)
     half = half_ref[0]
     receivers = all_ref[:, pl.ds(pl.multiple_of(half * 512, 512), 512)]
-    chosen = jnp.dot(every.astype(BF16), one_hot_ref[...], preferred_element_type=F32)
+    gathered = jnp.concatenate([stacked[16 * y : 16 * (y + 1)] for y in range(4)], axis=1)
+    chosen = jnp.dot(gathered, one_hot_ref[...], preferred_element_type=F32)
     even = iota(receivers.shape, 0) % 2 == 0
     turned = jnp.where(even, pltpu.roll(receivers, 15, 0), -pltpu.roll(receivers, 1, 0))
     chosen_t = chosen.T
@@ -265,43 +282,56 @@
 PARAMS = pltpu.CompilerParams(vmem_limit_bytes=32 * 1024 * 1024)
 
 
-def prepare(conv_weight, in_weight, out_weight, sources, raw, flags):
+def pack(raw, flags):
+    raw, flags = (pltpu.with_memory_space_constraint(a, pltpu.HBM) for a in (raw, flags))
+    return pl.pallas_call(
+        pack_kernel,
+        out_shape=jax.ShapeDtypeStruct((WIN, OWN, NT + LANES), BF16),
+        in_specs=[pl.BlockSpec(memory_space=pl.ANY)] * 2,
+        out_specs=VMEM,
+        scratch_shapes=[pltpu.VMEM(flags.shape, flags.dtype), pltpu.SemaphoreType.DMA((2,))],
+        compiler_params=PARAMS,
+        name="pack",
+    )(raw, flags)
+
+
+def prepare(cut, conv_weight, in_weight, out_weight, sources):
     arrays = (
         conv_weight.transpose(0, 3, 4, 1, 2), in_weight.T, out_weight.reshape(1, F), sources.reshape(1, NV),
-        raw, flags, jnp.asarray(sample_perm()), jnp.asarray(dft_table()), jnp.asarray(channel_perm()),
+        jnp.asarray(sample_perm()), jnp.asarray(dft_table()), jnp.asarray(channel_perm()),
     )
     arrays = tuple(pltpu.with_memory_space_constraint(a, pltpu.HBM) for a in arrays)
     return pl.pallas_call(
         prepare_kernel,
         out_shape=(
-            jax.ShapeDtypeStruct((LAYERS, BLK * F, 3 * 256), BF16),
-            jax.ShapeDtypeStruct((EXT * F, 72), BF16),
+            jax.ShapeDtypeStruct((LAYERS, 2, BLK * F, 3 * 256), BF16),
+            jax.ShapeDtypeStruct((EXT * F, 48), BF16),
             jax.ShapeDtypeStruct((OWN, OWN * F), BF16),
             jax.ShapeDtypeStruct((CH_ALL, NV), BF16),
         )
         + tuple(jax.ShapeDtypeStruct(a.shape, a.dtype) for a in arrays[4:]),
-        in_specs=[pl.BlockSpec(memory_space=pl.ANY)] * 9,
-        out_specs=(VMEM,) * 9,
+        in_specs=[SMEM] + [pl.BlockSpec(memory_space=pl.ANY)] * 7,
+        out_specs=(VMEM,) * 7,
         scratch_shapes=[pltpu.VMEM(a.shape, a.dtype) for a in arrays[:4]]
-        + [pltpu.SemaphoreType.DMA((9,))],
+        + [pltpu.SemaphoreType.DMA((7,))],
         compiler_params=PARAMS,
         cost_estimate=pl.CostEstimate(flops=2_000_000, bytes_accessed=4_000_000, transcendentals=0),
         name="prepare",
-    )(*arrays)
-
-
-def denoise(edge, far, raw, near, flags, order, band, first, last, table):
+    )(cut, *arrays)
+
+
+def denoise(own, left, order, band, first, last, table):
     return pl.pallas_call(
         denoise_kernel,
         out_shape=jax.ShapeDtypeStruct((64, 128), BF16),
-        in_specs=[SMEM] + [VMEM] * 9,
+        in_specs=[VMEM] * 7,
         out_specs=VMEM,
         scratch_shapes=[pltpu.VMEM(((EXT - 2 * i) * F, WIDE), BF16) for i in range(LAYERS + 1)]
         + [pltpu.VMEM((EXT * F, WIDE), BF16)] * 2
         + [pltpu.VMEM((64, 128), F32)],
         compiler_params=PARAMS,
         name="denoise",
-    )(edge, far, raw, near, flags, order, band, first, last, table)
+    )(own, left, order, band, first, last, table)
 
 
 def turn(rows):
@@ -336,17 +366,12 @@
 
 def per_device(raw, flags, in_weight, conv_weight, out_weight, sources):
     count = lax.axis_size(CHAN)
-    me = lax.axis_index(CHAN)
-    odd = lax.axis_index("c")
-    across = [(i, i + 1) for i in range(1, count - 1, 2)]
-    near = lax.ppermute(raw, "c", [(0, 1), (1, 0)])
-    far = lax.ppermute(raw, CHAN, across + [(b, a) for a, b in across])
-    edge = jnp.stack([me == 0, me == count - 1, odd == 1]).astype(jnp.int32)
+    own = pack(raw, flags)
+    left = lax.ppermute(own, CHAN, [(i, (i + 1) % count) for i in range(count)])
+    cut = (lax.axis_index(CHAN) == 0).astype(jnp.int32).reshape(1)
     half = lax.axis_index("w").reshape(1).astype(jnp.int32)
-    band, first, last, one_hot, raw, flags, order, table, perm = prepare(
-        conv_weight, in_weight, out_weight, sources, raw, flags
-    )
-    sent = denoise(edge, far, raw, near, flags, order, band, first, last, table)
+    band, first, last, one_hot, order, table, perm = prepare(cut, conv_weight, in_weight, out_weight, sources)
+    sent = denoise(own, left, order, band, first, last, table)
     half, sent = lax.optimization_barrier((half, sent))
     got = lax.all_to_all(
         sent, "z", 0, 0, tiled=True, axis_index_groups=[[int(z) for z in Z_ORDER]]

time: 47.5 us -> 47.9 us (level)
  starting transfers between devices: 9.44 us -> 4.94 us
  waiting for transfers between devices: 0.01 us -> 2.93 us
  Pallas kernels: 7.47 us -> 8.65 us
  blocking collectives: 30.2 us -> 31.1 us
    ppermute x2 -> x1, starting transfers between devices: 9.44 us -> 4.94 us  [per_device(): left = lax.ppermute(own, CHAN, [(i, (i + 1) % count) for i in range(count)])]
    ppermute x2 -> x1, waiting for transfers between devices: 0.01 us -> 2.93 us  [per_device(): left = lax.ppermute(own, CHAN, [(i, (i + 1) % count) for i in range(count)])]
    all_to_all x1, blocking collectives: 12.8 us -> 15.5 us  [per_device(): lax.all_to_all(turn(got), ('w', 'c', 'y', 's'), 0, 0, tiled=True, axis_in...]
    all_to_all x1, blocking collectives: 17.4 us -> 15.6 us  [per_device(): lax.all_to_all(sent, 'z', 0, 0, tiled=True, axis_index_groups=[[int(z) fo...]
    pallas_call x1 -> x2, Pallas kernels: 1.62 us -> 2.36 us  [the longest x1 1.58 us: prepare(): pl.pallas_call(prepare_kernel, out_shape=(jax.ShapeDtypeStruct((LAYERS, 2...]
    pallas_call x1, Pallas kernels: 4.21 us -> 4.77 us  [denoise(): pl.pallas_call(denoise_kernel, out_shape=jax.ShapeDtypeStruct((64, 128),...]
  transfers between devices with their start and end apart: 2 -> 1, of which waited for: 0 -> 1; matrix products, arithmetic and copies ran while one was open for 0% -> 0% of each run, Pallas kernels for 3% -> 3%
where the time goes in v4:
time: 47.9 us; the launch traced here: 47.6 us
  blocking collectives  31.1 us (65%)
  Pallas kernels  8.65 us (18%)
  starting transfers between devices  4.94 us (10%)
  waiting for transfers between devices  2.93 us (6%)
    all_to_all x1, blocking collectives, per_device(): lax.all_to_all(sent, 'z', 0, 0, tiled=True, axis_index_groups=[[int(z) fo...  15.6 us
    all_to_all x1, blocking collectives, per_device(): lax.all_to_all(turn(got), ('w', 'c', 'y', 's'), 0, 0, tiled=True, axis_in...  15.5 us
    ppermute x1, starting transfers between devices, per_device(): left = lax.ppermute(own, CHAN, [(i, (i + 1) % count) for i in range(count)])  4.94 us
    pallas_call x1, Pallas kernels, denoise(): pl.pallas_call(denoise_kernel, out_shape=jax.ShapeDtypeStruct((64, 128),...  4.77 us
    ppermute x1, waiting for transfers between devices, per_device(): left = lax.ppermute(own, CHAN, [(i, (i + 1) % count) for i in range(count)])  2.93 us
    pallas_call x1, Pallas kernels, prepare(): pl.pallas_call(prepare_kernel, out_shape=(jax.ShapeDtypeStruct((LAYERS, 2...  1.58 us
    pallas_call x1, Pallas kernels, coherence(): pl.pallas_call(coherence_kernel, out_shape=jax.ShapeDtypeStruct((1, 2, 12...  1.22 us
  transfers between devices with their start and end apart: 1, of which 1 were waited for; matrix products, arithmetic and copies ran while one was open for 0% of the time, Pallas kernels for 3%

profile of v4, /device:TPU:1, one launch (start us, length us, event | category | flops | bytes accessed | tf_op | source)
XLA Modules:
  0.0 47.6 jit_solution(11519170298741925106)
XLA Ops:
  0.0 0.8 %pack.1.own_ref = bf16[2,8,768]{2,1,0:T(8,128)(2,1)S(1)} custom-call(bf16[2,8,640]{2,1,0:T(8,128)(2,1)} %raw_any.1, s32[2,8]{1,0:T(2,128)} %flags_any.1), custom_call_target="tpu_custom_call" | custom-call | tf_op jit(solution)/shard_map/pack/pallas_call | solution.py:287
  0.8 4.9 %collective-permute-start = (bf16[2,8,768]{2,1,0:T(8,128)(2,1)S(1)}, bf16[2,8,768]{2,1,0:T(8,128)(2,1)S(1)}, u32[]{:S(2)}, u32[]{:S(2)}) collective-permute-start(bf16[2,8,768]{2,1,0:T(8,128)(2,1)S(1)} %pack.1.own_ref), channel_id=1, source_target_pairs={{0,2},{2,4},{4,6},{6,8},{8,10},{10,12},{12,14},{14,16},{16,18},{18... | collective-permute-start | bytes 73736 | tf_op jit(solution)/shard_map/ppermute | solution.py:370
  5.7 1.6 %prepare.1 = (bf16[3,2,192,768]{3,2,1,0:T(8,128)(2,1)S(1)}, bf16[448,48]{1,0:T(8,128)(2,1)S(1)}, bf16[8,256]{1,0:T(8,128)(2,1)S(1)}, bf16[1024,128]{1,0:T(8,128)...) custom-call(s32[1]{0:T(128)} %bitcast.1.cut_ref, ...), custom_call_target="tpu_custom_call" | custom-call | flops 2000000 | bytes 4000000 | tf_op jit(solution)/shard_map/prepare/pallas_call | solution.py:304
  7.3 2.9 %collective-permute-done.left_ref = bf16[2,8,768]{2,1,0:T(8,128)(2,1)S(1)} collective-permute-done((bf16[2,8,768]{2,1,0:T(8,128)(2,1)S(1)}, bf16[2,8,768]{2,1,0:T(8,128)(2,1)S(1)}, u32[]{:S(2)}, u32[]{:S(2)}) %collective-permute-start) | collective-permute-done | bytes 24608 | tf_op jit(solution)/shard_map/ppermute | solution.py:370
  10.3 4.8 %denoise.1 = bf16[64,128]{1,0:T(8,128)(2,1)S(1)} custom-call(bf16[2,8,768]{2,1,0:T(8,128)(2,1)S(1)} %pack.1.own_ref, bf16[2,8,768]{2,1,0:T(8,128)(2,1)S(1)} %collective-permute-done.left_ref, bf16[640,640]{1,0:T(8,128)(2,1)S(1)} %get-tuple-element.14.order_ref, bf16[3,2,192,768]{3,2,1,0:T(8,128)(2,1)S(1)} %get-tuple-element.15.band_ref, ...), custom_call_target="tpu_custom_call" | custom-call | tf_op jit(solution)/shard_map/denoise/pallas_call | solution.py:324
  15.0 15.6 %all_to_all.22 = bf16[16,4,128]{2,1,0:T(4,128)(2,1)S(1)} all-to-all(bf16[16,4,128]{2,1,0:T(4,128)(2,1)S(1)} %bitcast.12), channel_id=1, replica_groups={{32,36,40,44,48,52,56,60,0,4,8,12,16,20,24,28},{33,37,41,45,49,53,57,61..., dimensions={0} | all-to-all | bytes 32768 | tf_op jit(solution)/shard_map/all_to_all | solution.py:376
  30.6 0.3 turn.1
  30.9 15.5 %all_to_all.23 = bf16[32,4,128]{2,1,0:T(4,128)(2,1)S(1)} all-to-all(bf16[32,4,128]{2,1,0:T(4,128)(2,1)S(1)} %bitcast.11), channel_id=1, replica_groups={{129,385,193,449,1,257,65,321,131,387,195,451,3,259,67,323,128,384,192,..., dimensions={0} | all-to-all | bytes 65536 | tf_op jit(solution)/shard_map/all_to_all | solution.py:380
  46.4 1.2 %coherence.1 = f32[1,2,128,512]{3,2,1,0:T(8,128)} custom-call(s32[1]{0:T(128)} %bitcast.half_ref, bf16[1024,128]{1,0:T(8,128)(2,1)S(1)} %get-tuple-element.20.one_hot_ref, bf16[256,256]{1,0:T(8,128)(2,1)S(1)} %get-tuple-element.21.perm_ref, bf16[128,128]{1,0:T(8,128)(2,1)S(1)} %bitcast.10), custom_call_target="tpu_custom_call" | custom-call | tf_op jit(solution)/shard_map/coherence/pallas_call | solution.py:349
Async XLA Ops:
  0.8 9.5 %collective-permute-start = (bf16[2,8,768]{2,1,0:T(8,128)(2,1)S(1)}, bf16[2,8,768]{2,1,0:T(8,128)(2,1)S(1)}, u32[]{:S(2)}, u32[]{:S(2)}) collective-permute-start(bf16[2,8,768]{2,1,0:T(8,128)(2,1)S(1)} %pack.1.own_ref), channel_id=1, source_target_pairs={{0,2},{2,4},{4,6},{6,8},{8,10},{10,12},{12,14},{14,16},{16,18},{18... | collective-permute-start | bytes 73736 | tf_op jit(solution)/shard_map/ppermute | solution.py:370

commit v5 on v4

--- a/solution.py
+++ b/solution.py
@@ -123,7 +123,7 @@
     ).astype(BF16)
     copies[3].wait()
     shape = (CH_ALL, NV)
-    j = (sources_ref[...] + OWN // 2) % CH_ALL
+    j = (sources_ref[...] + CH_ALL - OWN // 2) % CH_ALL
     z = ((j // 16) % 16 - Z_ORDER[0]) % 16
     row = (j // 256) * 256 + ((j // 8) % 2) * 128 + (j % 8) * 16 + z
     one_hot_ref[...] = jnp.where(iota(shape, 0) == jnp.broadcast_to(row, shape), 1.0, 0.0).astype(BF16)
@@ -162,10 +162,10 @@
 
 
 def denoise_kernel(
-    own_ref, left_ref, order_ref, band_ref, first_ref, last_ref, table_ref,
+    after_ref, own_ref, order_ref, band_ref, first_ref, last_ref, table_ref,
     out_ref, h0_ref, h1_ref, h2_ref, h3_ref, earlier_ref, later_ref, line_ref,
 ):
-    rows = [ref[w, :, :NT].astype(F32) for w in range(WIN) for ref in (own_ref, left_ref)]
+    rows = [ref[w, :, :NT].astype(F32) for w in range(WIN) for ref in (after_ref, own_ref)]
     rows = jnp.concatenate(rows, axis=0).astype(BF16)
     rows = jnp.dot(rows, order_ref[...], preferred_element_type=F32)
     lines = [
@@ -181,7 +181,6 @@
         after = lines[v + 1] if v < PH - 1 else lane_shift(lines[0], -1)
         taps = jnp.concatenate([before, lines[v], after], axis=0).astype(BF16)
         h0_ref[:, chunk[v]] = jnp.dot(first_ref[...], taps, preferred_element_type=F32).astype(BF16)
-    spectra = None
     for layer in range(LAYERS):
         step = 2**layer
         source, target = hidden[layer], hidden[layer + 1]
@@ -203,12 +202,20 @@
                 total = jnp.dot(band_ref[layer, block, low * F :, :], taps, preferred_element_type=F32)
                 old = source[(start + low + 1) * F : (start + BLK + 1) * F, chunk[v]].astype(F32)
                 new = old + jnp.maximum(total, 0.0)
-                target[(start + low) * F : (start + BLK) * F, chunk[v]] = new.astype(BF16)
-            if layer == LAYERS - 1:
-                clean = jnp.dot(last_ref[...], target[:, chunk[v]], preferred_element_type=F32)
-                clean = jnp.concatenate([clean[:, :LANES], clean[:, LANES:]], axis=0).astype(BF16)
-                term = jnp.dot(clean, table_ref[v * LANES : (v + 1) * LANES, :], preferred_element_type=F32)
-                spectra = term if spectra is None else spectra + term
+                for i in range(BLK - low):
+                    c = start + low + i
+                    target[c * F : (c + 1) * F, chunk[v]] = new[i * F : (i + 1) * F].astype(BF16)
+    clean = jnp.dot(last_ref[...], h3_ref[...], preferred_element_type=F32)
+    clean = jnp.concatenate(
+        [
+            jnp.concatenate(
+                [clean[:, v * CHUNK + w * LANES : v * CHUNK + (w + 1) * LANES] for v in range(PH)], axis=1
+            )
+            for w in range(WIN)
+        ],
+        axis=0,
+    )
+    spectra = jnp.dot(clean.astype(BF16), table_ref[...], preferred_element_type=F32)
     real, imag = spectra[:, :NF], spectra[:, NF:]
     power = real * real + imag * imag
     spread = jnp.sqrt(jnp.mean(power, axis=1, keepdims=True) + epsilon_power)
@@ -216,7 +223,7 @@
         [
             ref[w, :, NT : NT + 1].astype(F32)[part]
             for w in range(WIN)
-            for ref, part in ((left_ref, slice(4, 8)), (own_ref, slice(0, 4)))
+            for ref, part in ((own_ref, slice(4, 8)), (after_ref, slice(0, 4)))
         ],
         axis=0,
     )
@@ -256,7 +263,7 @@
     ).astype(BF16)
     ordered = jnp.dot(stacked, perm_ref[...], preferred_element_type=F32)
     every = jnp.concatenate([ordered[16 * y : 16 * (y + 1)] for y in range(4)], axis=1)
-    all_ref[...] = pltpu.roll(every, CH_ALL - OWN // 2, 1)
+    all_ref[...] = pltpu.roll(every, OWN // 2, 1)
     half = half_ref[0]
     receivers = all_ref[:, pl.ds(pl.multiple_of(half * 512, 512), 512)]
     gathered = jnp.concatenate([stacked[16 * y : 16 * (y + 1)] for y in range(4)], axis=1)
@@ -320,7 +327,7 @@
     )(cut, *arrays)
 
 
-def denoise(own, left, order, band, first, last, table):
+def denoise(after, own, order, band, first, last, table):
     return pl.pallas_call(
         denoise_kernel,
         out_shape=jax.ShapeDtypeStruct((64, 128), BF16),
@@ -331,7 +338,7 @@
         + [pltpu.VMEM((64, 128), F32)],
         compiler_params=PARAMS,
         name="denoise",
-    )(own, left, order, band, first, last, table)
+    )(after, own, order, band, first, last, table)
 
 
 def turn(rows):
@@ -367,11 +374,11 @@
 def per_device(raw, flags, in_weight, conv_weight, out_weight, sources):
     count = lax.axis_size(CHAN)
     own = pack(raw, flags)
-    left = lax.ppermute(own, CHAN, [(i, (i + 1) % count) for i in range(count)])
-    cut = (lax.axis_index(CHAN) == 0).astype(jnp.int32).reshape(1)
+    after = lax.ppermute(own, CHAN, [((i + 1) % count, i) for i in range(count)])
+    cut = (lax.axis_index(CHAN) == count - 1).astype(jnp.int32).reshape(1)
     half = lax.axis_index("w").reshape(1).astype(jnp.int32)
     band, first, last, one_hot, order, table, perm = prepare(cut, conv_weight, in_weight, out_weight, sources)
-    sent = denoise(own, left, order, band, first, last, table)
+    sent = denoise(after, own, order, band, first, last, table)
     half, sent = lax.optimization_barrier((half, sent))
     got = lax.all_to_all(
         sent, "z", 0, 0, tiled=True, axis_index_groups=[[int(z) for z in Z_ORDER]]

time: 47.9 us -> 47 us (0.981)
  starting transfers between devices: 4.94 us -> 8.79 us
  waiting for transfers between devices: 2.93 us -> 0.01 us
  Pallas kernels: 8.65 us -> 7.65 us
  blocking collectives: 31.1 us -> 30.2 us
    ppermute x1, starting transfers between devices: 4.94 us -> 8.79 us  [per_device(): lax.ppermute(own, CHAN, [((i + 1) % count, i) for i in range(count)])]
    all_to_all x1, blocking collectives: 15.5 us -> 12.4 us  [per_device(): lax.all_to_all(turn(got), ('w', 'c', 'y', 's'), 0, 0, tiled=True, axis_in...]
    ppermute x1, waiting for transfers between devices: 2.93 us -> 0.01 us  [per_device(): lax.ppermute(own, CHAN, [((i + 1) % count, i) for i in range(count)])]
    all_to_all x1, blocking collectives: 15.6 us -> 17.8 us  [per_device(): lax.all_to_all(sent, 'z', 0, 0, tiled=True, axis_index_groups=[[int(z) fo...]
    pallas_call x1, Pallas kernels: 4.77 us -> 3.78 us  [denoise(): pl.pallas_call(denoise_kernel, out_shape=jax.ShapeDtypeStruct((64, 128),...]
  transfers between devices with their start and end apart: 1 -> 1, of which waited for: 1 -> 0; matrix products, arithmetic and copies ran while one was open for 0% -> 0% of each run, Pallas kernels for 3% -> 3%
where the time goes in v5:
time: 47 us; the launch traced here: 46.7 us
  blocking collectives  30.2 us (64%)
  starting transfers between devices  8.79 us (19%)
  Pallas kernels  7.65 us (16%)
    all_to_all x1, blocking collectives, per_device(): lax.all_to_all(sent, 'z', 0, 0, tiled=True, axis_index_groups=[[int(z) fo...  17.8 us
    all_to_all x1, blocking collectives, per_device(): lax.all_to_all(turn(got), ('w', 'c', 'y', 's'), 0, 0, tiled=True, axis_in...  12.4 us
    ppermute x1, starting transfers between devices, per_device(): lax.ppermute(own, CHAN, [((i + 1) % count, i) for i in range(count)])  8.79 us
    pallas_call x1, Pallas kernels, denoise(): pl.pallas_call(denoise_kernel, out_shape=jax.ShapeDtypeStruct((64, 128),...  3.78 us
    pallas_call x1, Pallas kernels, prepare(): pl.pallas_call(prepare_kernel, out_shape=(jax.ShapeDtypeStruct((LAYERS, 2...  1.58 us
    pallas_call x1, Pallas kernels, coherence(): pl.pallas_call(coherence_kernel, out_shape=jax.ShapeDtypeStruct((1, 2, 12...  1.22 us
  transfers between devices with their start and end apart: 1, of which 0 were waited for; matrix products, arithmetic and copies ran while one was open for 0% of the time, Pallas kernels for 3%

profile of v5, /device:TPU:1, one launch (start us, length us, event | category | flops | bytes accessed | tf_op | source)
XLA Modules:
  0.0 46.7 jit_solution(17605941739959569621)
XLA Ops:
  0.0 0.8 %pack.1.own_ref = bf16[2,8,768]{2,1,0:T(8,128)(2,1)S(1)} custom-call(bf16[2,8,640]{2,1,0:T(8,128)(2,1)} %raw_any.1, s32[2,8]{1,0:T(2,128)} %flags_any.1), custom_call_target="tpu_custom_call" | custom-call | tf_op jit(solution)/shard_map/pack/pallas_call | solution.py:294
  0.8 8.8 %collective-permute-start = (bf16[2,8,768]{2,1,0:T(8,128)(2,1)S(1)}, bf16[2,8,768]{2,1,0:T(8,128)(2,1)S(1)}, u32[]{:S(2)}, u32[]{:S(2)}) collective-permute-start(bf16[2,8,768]{2,1,0:T(8,128)(2,1)S(1)} %pack.1.own_ref), channel_id=1, source_target_pairs={{2,0},{4,2},{6,4},{8,6},{10,8},{12,10},{14,12},{16,14},{18,16},{20... | collective-permute-start | bytes 73736 | tf_op jit(solution)/shard_map/ppermute | solution.py:377
  9.6 1.6 %prepare.1 = (bf16[3,2,192,768]{3,2,1,0:T(8,128)(2,1)S(1)}, bf16[448,48]{1,0:T(8,128)(2,1)S(1)}, bf16[8,256]{1,0:T(8,128)(2,1)S(1)}, bf16[1024,128]{1,0:T(8,128)...) custom-call(s32[1]{0:T(128)} %bitcast.1.cut_ref, ...), custom_call_target="tpu_custom_call" | custom-call | flops 2000000 | bytes 4000000 | tf_op jit(solution)/shard_map/prepare/pallas_call | solution.py:311
  11.2 0.0 collective-permute-done.after_ref
  11.2 3.8 %denoise.1 = bf16[64,128]{1,0:T(8,128)(2,1)S(1)} custom-call(bf16[2,8,768]{2,1,0:T(8,128)(2,1)S(1)} %collective-permute-done.after_ref, bf16[2,8,768]{2,1,0:T(8,128)(2,1)S(1)} %pack.1.own_ref, bf16[640,640]{1,0:T(8,128)(2,1)S(1)} %get-tuple-element.14.order_ref, bf16[3,2,192,768]{3,2,1,0:T(8,128)(2,1)S(1)} %get-tuple-element.15.band_ref, ...), custom_call_target="tpu_custom_call" | custom-call | tf_op jit(solution)/shard_map/denoise/pallas_call | solution.py:331
  15.0 17.8 %all_to_all.22 = bf16[16,4,128]{2,1,0:T(4,128)(2,1)S(1)} all-to-all(bf16[16,4,128]{2,1,0:T(4,128)(2,1)S(1)} %bitcast.12), channel_id=1, replica_groups={{32,36,40,44,48,52,56,60,0,4,8,12,16,20,24,28},{33,37,41,45,49,53,57,61..., dimensions={0} | all-to-all | bytes 32768 | tf_op jit(solution)/shard_map/all_to_all | solution.py:383
  32.8 0.3 turn.1
  33.1 12.4 %all_to_all.23 = bf16[32,4,128]{2,1,0:T(4,128)(2,1)S(1)} all-to-all(bf16[32,4,128]{2,1,0:T(4,128)(2,1)S(1)} %bitcast.11), channel_id=1, replica_groups={{129,385,193,449,1,257,65,321,131,387,195,451,3,259,67,323,128,384,192,..., dimensions={0} | all-to-all | bytes 65536 | tf_op jit(solution)/shard_map/all_to_all | solution.py:387
  45.5 1.2 %coherence.1 = f32[1,2,128,512]{3,2,1,0:T(8,128)} custom-call(s32[1]{0:T(128)} %bitcast.half_ref, bf16[1024,128]{1,0:T(8,128)(2,1)S(1)} %get-tuple-element.20.one_hot_ref, bf16[256,256]{1,0:T(8,128)(2,1)S(1)} %get-tuple-element.21.perm_ref, bf16[128,128]{1,0:T(8,128)(2,1)S(1)} %bitcast.10), custom_call_target="tpu_custom_call" | custom-call | tf_op jit(solution)/shard_map/coherence/pallas_call | solution.py:356
Async XLA Ops:
  0.8 10.4 %collective-permute-start = (bf16[2,8,768]{2,1,0:T(8,128)(2,1)S(1)}, bf16[2,8,768]{2,1,0:T(8,128)(2,1)S(1)}, u32[]{:S(2)}, u32[]{:S(2)}) collective-permute-start(bf16[2,8,768]{2,1,0:T(8,128)(2,1)S(1)} %pack.1.own_ref), channel_id=1, source_target_pairs={{2,0},{4,2},{6,4},{8,6},{10,8},{12,10},{14,12},{16,14},{18,16},{20... | collective-permute-start | bytes 73736 | tf_op jit(solution)/shard_map/ppermute | solution.py:377

commit v6 on v5

--- a/solution.py
+++ b/solution.py
@@ -78,43 +78,56 @@
     return jnp.where(row_bit == lane_bit, x, jnp.where(row_bit == 0, down, up))
 
 
-def pack_kernel(raw_any, flags_any, own_ref, flags_ref, sems):
-    copies = (
-        pltpu.make_async_copy(flags_any, flags_ref, sems.at[0]),
-        pltpu.make_async_copy(raw_any, own_ref.at[:, :, pl.ds(0, NT)], sems.at[1]),
-    )
-    for copy in copies:
-        copy.start()
-    copies[0].wait()
-    for w in range(WIN):
-        flags = column(flags_ref[w : w + 1, :].astype(F32), OWN)
-        own_ref[w, :, NT:] = jnp.broadcast_to(flags, (OWN, LANES)).astype(BF16)
-    copies[1].wait()
+def lane_shift(x, step):
+    edge = iota((x.shape[0], LANES), 1) == (0 if step == 1 else LANES - 1)
+    moved = [
+        jnp.where(edge, jnp.zeros_like(part), pltpu.roll(part, step % LANES, 1))
+        for part in (x[:, i : i + LANES] for i in range(0, x.shape[1], LANES))
+    ]
+    return jnp.concatenate(moved, axis=1)
+
+
+def input_layer(rows, order, weights, put):
+    rows = jnp.concatenate([rows[w].astype(F32) for w in range(WIN)], axis=0).astype(BF16)
+    rows = jnp.dot(rows, order, preferred_element_type=F32)
+    lines = [
+        jnp.concatenate(
+            [rows[OWN * w : OWN * (w + 1), v * LANES : (v + 1) * LANES] for w in range(WIN)], axis=1
+        )
+        for v in range(PH)
+    ]
+    for v in range(PH):
+        before = lines[v - 1] if v > 0 else lane_shift(lines[PH - 1], 1)
+        after = lines[v + 1] if v < PH - 1 else lane_shift(lines[0], -1)
+        taps = jnp.concatenate([before, lines[v], after], axis=0).astype(BF16)
+        put(v, jnp.dot(weights, taps, preferred_element_type=F32).astype(BF16))
 
 
 def prepare_kernel(
-    cut_ref, conv_any, in_any, out_any, sources_any, order_any, table_any, perm_any,
-    band_ref, first_ref, last_ref, one_hot_ref, order_ref, table_ref, perm_ref,
+    cut_ref, conv_any, in_any, out_any, sources_any, raw_any, order_any, flags_any, perm_any,
+    band_ref, first_ref, last_ref, one_hot_ref, raw_ref, order_ref, flags_ref, perm_ref,
     conv_ref, in_ref, out_ref, sources_ref, sems,
 ):
     pairs = (
         (conv_any, conv_ref), (in_any, in_ref), (out_any, out_ref), (sources_any, sources_ref),
-        (order_any, order_ref), (table_any, table_ref), (perm_any, perm_ref),
+        (raw_any, raw_ref), (order_any, order_ref), (flags_any, flags_ref), (perm_any, perm_ref),
     )
     copies = [pltpu.make_async_copy(a, b, sems.at[i]) for i, (a, b) in enumerate(pairs)]
     for copy in copies:
         copy.start()
     copies[1].wait()
-    shape = (EXT * F, 48)
-    channel = iota(shape, 0) // F
-    place = jnp.where(channel < 7, OWN + 1 + channel, channel - 7)
-    lane = iota(shape, 1)
-    first = jnp.zeros(shape, F32)
+    half = EXT // 2
+    shape = (half * F, 3 * OWN)
+    channel, lane = iota(shape, 0) // F, iota(shape, 1)
+    talls = []
     for tap in range(3):
         weight = column(in_ref[tap : tap + 1, :].astype(F32), F)
-        tall = jnp.broadcast_to(jnp.concatenate([weight] * EXT, axis=0), shape)
-        first = jnp.where(lane == place + 16 * tap, tall, first)
-    first_ref[...] = first.astype(BF16)
+        talls.append(jnp.broadcast_to(jnp.concatenate([weight] * half, axis=0), shape))
+    for i, place in enumerate((channel + 1, channel)):
+        first = jnp.zeros(shape, F32)
+        for tap in range(3):
+            first = jnp.where(lane == place + OWN * tap, talls[tap], first)
+        first_ref[i] = first.astype(BF16)
     copies[2].wait()
     shape = (OWN, OWN * F)
     wide = jnp.concatenate([out_ref[...].astype(F32)] * OWN, axis=1)
@@ -123,7 +136,7 @@
     ).astype(BF16)
     copies[3].wait()
     shape = (CH_ALL, NV)
-    j = (sources_ref[...] + CH_ALL - OWN // 2) % CH_ALL
+    j = (sources_ref[...] + OWN // 2) % CH_ALL
     z = ((j // 16) % 16 - Z_ORDER[0]) % 16
     row = (j // 256) * 256 + ((j // 8) % 2) * 128 + (j % 8) * 16 + z
     one_hot_ref[...] = jnp.where(iota(shape, 0) == jnp.broadcast_to(row, shape), 1.0, 0.0).astype(BF16)
@@ -152,35 +165,21 @@
         copy.wait()
 
 
-def lane_shift(x, step):
-    edge = iota((x.shape[0], LANES), 1) == (0 if step == 1 else LANES - 1)
-    moved = [
-        jnp.where(edge, jnp.zeros_like(part), pltpu.roll(part, step % LANES, 1))
-        for part in (x[:, i : i + LANES] for i in range(0, x.shape[1], LANES))
-    ]
-    return jnp.concatenate(moved, axis=1)
-
-
 def denoise_kernel(
-    after_ref, own_ref, order_ref, band_ref, first_ref, last_ref, table_ref,
-    out_ref, h0_ref, h1_ref, h2_ref, h3_ref, earlier_ref, later_ref, line_ref,
+    before_ref, before_flags_ref, raw_ref, flags_ref, order_ref, band_ref, first_ref, last_ref, table_any,
+    out_ref, h0_ref, h1_ref, h2_ref, h3_ref, earlier_ref, later_ref, line_ref, table_ref, sem,
 ):
-    rows = [ref[w, :, :NT].astype(F32) for w in range(WIN) for ref in (after_ref, own_ref)]
-    rows = jnp.concatenate(rows, axis=0).astype(BF16)
-    rows = jnp.dot(rows, order_ref[...], preferred_element_type=F32)
-    lines = [
-        jnp.concatenate(
-            [rows[16 * w : 16 * (w + 1), v * LANES : (v + 1) * LANES] for w in range(WIN)], axis=1
-        )
-        for v in range(PH)
-    ]
+    table_copy = pltpu.make_async_copy(table_any, table_ref, sem)
+    table_copy.start()
     hidden = (h0_ref, h1_ref, h2_ref, h3_ref)
     chunk = [slice(v * CHUNK, (v + 1) * CHUNK) for v in range(PH)]
-    for v in range(PH):
-        before = lines[v - 1] if v > 0 else lane_shift(lines[PH - 1], 1)
-        after = lines[v + 1] if v < PH - 1 else lane_shift(lines[0], -1)
-        taps = jnp.concatenate([before, lines[v], after], axis=0).astype(BF16)
-        h0_ref[:, chunk[v]] = jnp.dot(first_ref[...], taps, preferred_element_type=F32).astype(BF16)
+    for i, ref in enumerate((before_ref, raw_ref)):
+        rows = slice(i * EXT // 2 * F, (i + 1) * EXT // 2 * F)
+
+        def put(v, value, rows=rows):
+            h0_ref[rows, chunk[v]] = value
+
+        input_layer(ref, order_ref[...], first_ref[i], put)
     for layer in range(LAYERS):
         step = 2**layer
         source, target = hidden[layer], hidden[layer + 1]
@@ -215,15 +214,16 @@
         ],
         axis=0,
     )
+    table_copy.wait()
     spectra = jnp.dot(clean.astype(BF16), table_ref[...], preferred_element_type=F32)
     real, imag = spectra[:, :NF], spectra[:, NF:]
     power = real * real + imag * imag
     spread = jnp.sqrt(jnp.mean(power, axis=1, keepdims=True) + epsilon_power)
     flags = jnp.concatenate(
         [
-            ref[w, :, NT : NT + 1].astype(F32)[part]
+            column(ref[w : w + 1, :].astype(F32), OWN)[part]
             for w in range(WIN)
-            for ref, part in ((own_ref, slice(4, 8)), (after_ref, slice(0, 4)))
+            for ref, part in ((before_flags_ref, slice(4, 8)), (flags_ref, slice(0, 4)))
         ],
         axis=0,
     )
@@ -263,7 +263,7 @@
     ).astype(BF16)
     ordered = jnp.dot(stacked, perm_ref[...], preferred_element_type=F32)
     every = jnp.concatenate([ordered[16 * y : 16 * (y + 1)] for y in range(4)], axis=1)
-    all_ref[...] = pltpu.roll(every, OWN // 2, 1)
+    all_ref[...] = pltpu.roll(every, CH_ALL - OWN // 2, 1)
     half = half_ref[0]
     receivers = all_ref[:, pl.ds(pl.multiple_of(half * 512, 512), 512)]
     gathered = jnp.concatenate([stacked[16 * y : 16 * (y + 1)] for y in range(4)], axis=1)
@@ -286,59 +286,47 @@
 
 VMEM = pl.BlockSpec(memory_space=pltpu.VMEM)
 SMEM = pl.BlockSpec(memory_space=pltpu.SMEM)
-PARAMS = pltpu.CompilerParams(vmem_limit_bytes=32 * 1024 * 1024)
-
-
-def pack(raw, flags):
-    raw, flags = (pltpu.with_memory_space_constraint(a, pltpu.HBM) for a in (raw, flags))
-    return pl.pallas_call(
-        pack_kernel,
-        out_shape=jax.ShapeDtypeStruct((WIN, OWN, NT + LANES), BF16),
-        in_specs=[pl.BlockSpec(memory_space=pl.ANY)] * 2,
-        out_specs=VMEM,
-        scratch_shapes=[pltpu.VMEM(flags.shape, flags.dtype), pltpu.SemaphoreType.DMA((2,))],
-        compiler_params=PARAMS,
-        name="pack",
-    )(raw, flags)
-
-
-def prepare(cut, conv_weight, in_weight, out_weight, sources):
+PARAMS = pltpu.CompilerParams(vmem_limit_bytes=16 * 1024 * 1024)
+
+
+def prepare(cut, conv_weight, in_weight, out_weight, sources, raw, flags):
     arrays = (
         conv_weight.transpose(0, 3, 4, 1, 2), in_weight.T, out_weight.reshape(1, F), sources.reshape(1, NV),
-        jnp.asarray(sample_perm()), jnp.asarray(dft_table()), jnp.asarray(channel_perm()),
+        raw, jnp.asarray(sample_perm()), flags, jnp.asarray(channel_perm()),
     )
     arrays = tuple(pltpu.with_memory_space_constraint(a, pltpu.HBM) for a in arrays)
     return pl.pallas_call(
         prepare_kernel,
         out_shape=(
             jax.ShapeDtypeStruct((LAYERS, 2, BLK * F, 3 * 256), BF16),
-            jax.ShapeDtypeStruct((EXT * F, 48), BF16),
+            jax.ShapeDtypeStruct((2, EXT // 2 * F, 3 * OWN), BF16),
             jax.ShapeDtypeStruct((OWN, OWN * F), BF16),
             jax.ShapeDtypeStruct((CH_ALL, NV), BF16),
         )
         + tuple(jax.ShapeDtypeStruct(a.shape, a.dtype) for a in arrays[4:]),
-        in_specs=[SMEM] + [pl.BlockSpec(memory_space=pl.ANY)] * 7,
-        out_specs=(VMEM,) * 7,
+        in_specs=[SMEM] + [pl.BlockSpec(memory_space=pl.ANY)] * 8,
+        out_specs=(VMEM,) * 8,
         scratch_shapes=[pltpu.VMEM(a.shape, a.dtype) for a in arrays[:4]]
-        + [pltpu.SemaphoreType.DMA((7,))],
+        + [pltpu.SemaphoreType.DMA((8,))],
         compiler_params=PARAMS,
         cost_estimate=pl.CostEstimate(flops=2_000_000, bytes_accessed=4_000_000, transcendentals=0),
         name="prepare",
     )(cut, *arrays)
 
 
-def denoise(after, own, order, band, first, last, table):
+def denoise(before, before_flags, raw, flags, order, band, first, last):
+    table = pltpu.with_memory_space_constraint(jnp.asarray(dft_table()), pltpu.HBM)
     return pl.pallas_call(
         denoise_kernel,
         out_shape=jax.ShapeDtypeStruct((64, 128), BF16),
-        in_specs=[VMEM] * 7,
+        in_specs=[VMEM] * 8 + [pl.BlockSpec(memory_space=pl.ANY)],
         out_specs=VMEM,
         scratch_shapes=[pltpu.VMEM(((EXT - 2 * i) * F, WIDE), BF16) for i in range(LAYERS + 1)]
         + [pltpu.VMEM((EXT * F, WIDE), BF16)] * 2
-        + [pltpu.VMEM((64, 128), F32)],
+        + [pltpu.VMEM((64, 128), F32), pltpu.VMEM(table.shape, BF16), pltpu.SemaphoreType.DMA],
         compiler_params=PARAMS,
         name="denoise",
-    )(after, own, order, band, first, last, table)
+    )(before, before_flags, raw, flags, order, band, first, last, table)
 
 
 def turn(rows):
@@ -373,12 +361,15 @@
 
 def per_device(raw, flags, in_weight, conv_weight, out_weight, sources):
     count = lax.axis_size(CHAN)
-    own = pack(raw, flags)
-    after = lax.ppermute(own, CHAN, [((i + 1) % count, i) for i in range(count)])
-    cut = (lax.axis_index(CHAN) == count - 1).astype(jnp.int32).reshape(1)
+    ring = [(i, (i + 1) % count) for i in range(count)]
+    before = lax.ppermute(raw, CHAN, ring)
+    before_flags = lax.ppermute(flags, CHAN, ring)
+    cut = (lax.axis_index(CHAN) == 0).astype(jnp.int32).reshape(1)
     half = lax.axis_index("w").reshape(1).astype(jnp.int32)
-    band, first, last, one_hot, order, table, perm = prepare(cut, conv_weight, in_weight, out_weight, sources)
-    sent = denoise(after, own, order, band, first, last, table)
+    band, first, last, one_hot, raw, order, flags, perm = prepare(
+        cut, conv_weight, in_weight, out_weight, sources, raw, flags
+    )
+    sent = denoise(before, before_flags, raw, flags, order, band, first, last)
     half, sent = lax.optimization_barrier((half, sent))
     got = lax.all_to_all(
         sent, "z", 0, 0, tiled=True, axis_index_groups=[[int(z) for z in Z_ORDER]]

time: 47 us -> 48.9 us (1.040)
  waiting for transfers between devices: 0.01 us -> 3.15 us
  starting transfers between devices: 8.79 us -> 6.84 us
  blocking collectives: 30.2 us -> 30.9 us
    ppermute x1 -> x2, waiting for transfers between devices: 0.01 us -> 3.15 us  [the longest x1 3.15 us: per_device(): before_flags = lax.ppermute(flags, CHAN, ring)]
    all_to_all x1, blocking collectives: 12.4 us -> 15.5 us  [per_device(): lax.all_to_all(turn(got), ('w', 'c', 'y', 's'), 0, 0, tiled=True, axis_in...]
    all_to_all x1, blocking collectives: 17.8 us -> 15.4 us  [per_device(): lax.all_to_all(sent, 'z', 0, 0, tiled=True, axis_index_groups=[[int(z) fo...]
    ppermute x1 -> x2, starting transfers between devices: 8.79 us -> 6.84 us  [the longest x1 4.92 us: per_device(): before = lax.ppermute(raw, CHAN, ring)]
    pallas_call x1, Pallas kernels: 3.78 us -> 4.66 us  [denoise(): pl.pallas_call(denoise_kernel, out_shape=jax.ShapeDtypeStruct((64, 128),...]
    pallas_call x1 -> x0, Pallas kernels: 0.78 us -> none  [pack(): pl.pallas_call(pack_kernel, out_shape=jax.ShapeDtypeStruct((WIN, OWN, NT...]
  transfers between devices with their start and end apart: 1 -> 2, of which waited for: 0 -> 1; matrix products, arithmetic and copies ran while one was open for 0% -> 0% of each run, Pallas kernels for 3% -> 3%
where the time goes in v6:
time: 48.9 us; the launch traced here: 48.6 us
  blocking collectives  30.9 us (63%)
  Pallas kernels  7.68 us (16%)
  starting transfers between devices  6.84 us (14%)
  waiting for transfers between devices  3.15 us (6%)
    all_to_all x1, blocking collectives, per_device(): lax.all_to_all(turn(got), ('w', 'c', 'y', 's'), 0, 0, tiled=True, axis_in...  15.5 us
    all_to_all x1, blocking collectives, per_device(): lax.all_to_all(sent, 'z', 0, 0, tiled=True, axis_index_groups=[[int(z) fo...  15.4 us
    ppermute x1, starting transfers between devices, per_device(): before = lax.ppermute(raw, CHAN, ring)  4.92 us
    pallas_call x1, Pallas kernels, denoise(): pl.pallas_call(denoise_kernel, out_shape=jax.ShapeDtypeStruct((64, 128),...  4.66 us
    ppermute x1, waiting for transfers between devices, per_device(): before_flags = lax.ppermute(flags, CHAN, ring)  3.15 us
    ppermute x1, starting transfers between devices, per_device(): before_flags = lax.ppermute(flags, CHAN, ring)  1.92 us
    pallas_call x1, Pallas kernels, prepare(): pl.pallas_call(prepare_kernel, out_shape=(jax.ShapeDtypeStruct((LAYERS, 2...  1.51 us
    pallas_call x1, Pallas kernels, coherence(): pl.pallas_call(coherence_kernel, out_shape=jax.ShapeDtypeStruct((1, 2, 12...  1.22 us
  transfers between devices with their start and end apart: 2, of which 1 were waited for; matrix products, arithmetic and copies ran while one was open for 0% of the time, Pallas kernels for 3%

profile of v6, /device:TPU:1, one launch (start us, length us, event | category | flops | bytes accessed | tf_op | source)
XLA Modules:
  0.0 48.6 jit_solution(16954885146475556290)
XLA Ops:
  0.0 4.9 %collective-permute-start = (bf16[2,8,640]{2,1,0:T(8,128)(2,1)}, bf16[2,8,640]{2,1,0:T(8,128)(2,1)S(1)}, u32[]{:S(2)}, u32[]{:S(2)}) collective-permute-start(bf16[2,8,640]{2,1,0:T(8,128)(2,1)} %raw_any.1), channel_id=1, source_target_pairs={{0,2},{2,4},{4,6},{6,8},{8,10},{10,12},{12,14},{14,16},{16,18},{18... | collective-permute-start | bytes 61448 | tf_op jit(solution)/shard_map/ppermute | solution.py:365
  4.9 1.9 %collective-permute-start.1 = (s32[2,8]{1,0:T(2,128)}, s32[2,8]{1,0:T(2,128)S(1)}, u32[]{:S(2)}, u32[]{:S(2)}) collective-permute-start(s32[2,8]{1,0:T(2,128)} %flags_any.1), channel_id=1, source_target_pairs={{0,2},{2,4},{4,6},{6,8},{8,10},{10,12},{12,14},{14,16},{16,18},{18... | collective-permute-start | bytes 200 | tf_op jit(solution)/shard_map/ppermute | solution.py:366
  6.9 1.5 %prepare.1 = (bf16[3,2,192,768]{3,2,1,0:T(8,128)(2,1)S(1)}, bf16[2,224,24]{2,1,0:T(8,128)(2,1)S(1)}, bf16[8,256]{1,0:T(8,128)(2,1)S(1)}, bf16[1024,128]{1,0:T(8,...) custom-call(s32[1]{0:T(128)} %bitcast.1.cut_ref, ...), custom_call_target="tpu_custom_call" | custom-call | flops 2000000 | bytes 4000000 | tf_op jit(solution)/shard_map/prepare/pallas_call | solution.py:298
  8.4 3.2 %collective-permute-done.1.before_flags_ref = s32[2,8]{1,0:T(2,128)S(1)} collective-permute-done((s32[2,8]{1,0:T(2,128)}, s32[2,8]{1,0:T(2,128)S(1)}, u32[]{:S(2)}, u32[]{:S(2)}) %collective-permute-start.1) | collective-permute-done | bytes 96 | tf_op jit(solution)/shard_map/ppermute | solution.py:366
  11.5 0.0 collective-permute-done.before_ref
  11.5 4.7 %denoise.1 = bf16[64,128]{1,0:T(8,128)(2,1)S(1)} custom-call(bf16[2,8,640]{2,1,0:T(8,128)(2,1)S(1)} %collective-permute-done.before_ref, s32[2,8]{1,0:T(2,128)S(1)} %collective-permute-done.1.before_flags_ref, bf16[2,8,640]{2,1,0:T(8,128)(2,1)S(1)} %get-tuple-element.15.raw_ref, s32[2,8]{1,0:T(2,128)S(1)} %get-tuple-element.16.flags_ref, ...), custom_call_target="tpu_custom_call" | custom-call | tf_op jit(solution)/shard_map/denoise/pallas_call | solution.py:319
  16.2 15.4 %all_to_all.22 = bf16[16,4,128]{2,1,0:T(4,128)(2,1)S(1)} all-to-all(bf16[16,4,128]{2,1,0:T(4,128)(2,1)S(1)} %bitcast.12), channel_id=1, replica_groups={{32,36,40,44,48,52,56,60,0,4,8,12,16,20,24,28},{33,37,41,45,49,53,57,61..., dimensions={0} | all-to-all | bytes 32768 | tf_op jit(solution)/shard_map/all_to_all | solution.py:374
  31.6 0.3 turn.1
  31.9 15.5 %all_to_all.23 = bf16[32,4,128]{2,1,0:T(4,128)(2,1)S(1)} all-to-all(bf16[32,4,128]{2,1,0:T(4,128)(2,1)S(1)} %bitcast.11), channel_id=1, replica_groups={{129,385,193,449,1,257,65,321,131,387,195,451,3,259,67,323,128,384,192,..., dimensions={0} | all-to-all | bytes 65536 | tf_op jit(solution)/shard_map/all_to_all | solution.py:378
  47.4 1.2 %coherence.1 = f32[1,2,128,512]{3,2,1,0:T(8,128)} custom-call(s32[1]{0:T(128)} %bitcast.half_ref, bf16[1024,128]{1,0:T(8,128)(2,1)S(1)} %get-tuple-element.22.one_hot_ref, bf16[256,256]{1,0:T(8,128)(2,1)S(1)} %get-tuple-element.23.perm_ref, bf16[128,128]{1,0:T(8,128)(2,1)S(1)} %bitcast.10), custom_call_target="tpu_custom_call" | custom-call | tf_op jit(solution)/shard_map/coherence/pallas_call | solution.py:344
Async XLA Ops:
  0.0 11.5 %collective-permute-start = (bf16[2,8,640]{2,1,0:T(8,128)(2,1)}, bf16[2,8,640]{2,1,0:T(8,128)(2,1)S(1)}, u32[]{:S(2)}, u32[]{:S(2)}) collective-permute-start(bf16[2,8,640]{2,1,0:T(8,128)(2,1)} %raw_any.1), channel_id=1, source_target_pairs={{0,2},{2,4},{4,6},{6,8},{8,10},{10,12},{12,14},{14,16},{16,18},{18... | collective-permute-start | bytes 61448 | tf_op jit(solution)/shard_map/ppermute | solution.py:365
  4.9 6.6 %collective-permute-start.1 = (s32[2,8]{1,0:T(2,128)}, s32[2,8]{1,0:T(2,128)S(1)}, u32[]{:S(2)}, u32[]{:S(2)}) collective-permute-start(s32[2,8]{1,0:T(2,128)} %flags_any.1), channel_id=1, source_target_pairs={{0,2},{2,4},{4,6},{6,8},{8,10},{10,12},{12,14},{14,16},{16,18},{18... | collective-permute-start | bytes 200 | tf_op jit(solution)/shard_map/ppermute | solution.py:366

commit v7 on v5

--- a/solution.py
+++ b/solution.py
@@ -123,7 +123,7 @@
     ).astype(BF16)
     copies[3].wait()
     shape = (CH_ALL, NV)
-    j = (sources_ref[...] + CH_ALL - OWN // 2) % CH_ALL
+    j = (sources_ref[...] + OWN // 2) % CH_ALL
     z = ((j // 16) % 16 - Z_ORDER[0]) % 16
     row = (j // 256) * 256 + ((j // 8) % 2) * 128 + (j % 8) * 16 + z
     one_hot_ref[...] = jnp.where(iota(shape, 0) == jnp.broadcast_to(row, shape), 1.0, 0.0).astype(BF16)
@@ -162,10 +162,10 @@
 
 
 def denoise_kernel(
-    after_ref, own_ref, order_ref, band_ref, first_ref, last_ref, table_ref,
+    own_ref, left_ref, order_ref, band_ref, first_ref, last_ref, table_ref,
     out_ref, h0_ref, h1_ref, h2_ref, h3_ref, earlier_ref, later_ref, line_ref,
 ):
-    rows = [ref[w, :, :NT].astype(F32) for w in range(WIN) for ref in (after_ref, own_ref)]
+    rows = [ref[w, :, :NT].astype(F32) for w in range(WIN) for ref in (own_ref, left_ref)]
     rows = jnp.concatenate(rows, axis=0).astype(BF16)
     rows = jnp.dot(rows, order_ref[...], preferred_element_type=F32)
     lines = [
@@ -223,7 +223,7 @@
         [
             ref[w, :, NT : NT + 1].astype(F32)[part]
             for w in range(WIN)
-            for ref, part in ((own_ref, slice(4, 8)), (after_ref, slice(0, 4)))
+            for ref, part in ((left_ref, slice(4, 8)), (own_ref, slice(0, 4)))
         ],
         axis=0,
     )
@@ -263,7 +263,7 @@
     ).astype(BF16)
     ordered = jnp.dot(stacked, perm_ref[...], preferred_element_type=F32)
     every = jnp.concatenate([ordered[16 * y : 16 * (y + 1)] for y in range(4)], axis=1)
-    all_ref[...] = pltpu.roll(every, OWN // 2, 1)
+    all_ref[...] = pltpu.roll(every, CH_ALL - OWN // 2, 1)
     half = half_ref[0]
     receivers = all_ref[:, pl.ds(pl.multiple_of(half * 512, 512), 512)]
     gathered = jnp.concatenate([stacked[16 * y : 16 * (y + 1)] for y in range(4)], axis=1)
@@ -327,7 +327,7 @@
     )(cut, *arrays)
 
 
-def denoise(after, own, order, band, first, last, table):
+def denoise(own, left, order, band, first, last, table):
     return pl.pallas_call(
         denoise_kernel,
         out_shape=jax.ShapeDtypeStruct((64, 128), BF16),
@@ -338,7 +338,7 @@
         + [pltpu.VMEM((64, 128), F32)],
         compiler_params=PARAMS,
         name="denoise",
-    )(after, own, order, band, first, last, table)
+    )(own, left, order, band, first, last, table)
 
 
 def turn(rows):
@@ -374,11 +374,11 @@
 def per_device(raw, flags, in_weight, conv_weight, out_weight, sources):
     count = lax.axis_size(CHAN)
     own = pack(raw, flags)
-    after = lax.ppermute(own, CHAN, [((i + 1) % count, i) for i in range(count)])
-    cut = (lax.axis_index(CHAN) == count - 1).astype(jnp.int32).reshape(1)
+    left = lax.ppermute(own, CHAN, [(i, (i + 1) % count) for i in range(count)])
+    cut = (lax.axis_index(CHAN) == 0).astype(jnp.int32).reshape(1)
     half = lax.axis_index("w").reshape(1).astype(jnp.int32)
     band, first, last, one_hot, order, table, perm = prepare(cut, conv_weight, in_weight, out_weight, sources)
-    sent = denoise(after, own, order, band, first, last, table)
+    sent = denoise(own, left, order, band, first, last, table)
     half, sent = lax.optimization_barrier((half, sent))
     got = lax.all_to_all(
         sent, "z", 0, 0, tiled=True, axis_index_groups=[[int(z) for z in Z_ORDER]]

time: 47 us -> 46.9 us (level)
  starting transfers between devices: 8.79 us -> 4.94 us
  waiting for transfers between devices: 0.01 us -> 2.93 us
  blocking collectives: 30.2 us -> 31.1 us
    ppermute x1, starting transfers between devices: 8.79 us -> 4.94 us  [per_device(): left = lax.ppermute(own, CHAN, [(i, (i + 1) % count) for i in range(count)])]
    all_to_all x1, blocking collectives: 12.4 us -> 15.5 us  [per_device(): lax.all_to_all(turn(got), ('w', 'c', 'y', 's'), 0, 0, tiled=True, axis_in...]
    ppermute x1, waiting for transfers between devices: 0.01 us -> 2.93 us  [per_device(): left = lax.ppermute(own, CHAN, [(i, (i + 1) % count) for i in range(count)])]
    all_to_all x1, blocking collectives: 17.8 us -> 15.6 us  [per_device(): lax.all_to_all(sent, 'z', 0, 0, tiled=True, axis_index_groups=[[int(z) fo...]
  transfers between devices with their start and end apart: 1 -> 1, of which waited for: 0 -> 1; matrix products, arithmetic and copies ran while one was open for 0% -> 0% of each run, Pallas kernels for 3% -> 3%
where the time goes in v7:
time: 46.9 us; the launch traced here: 46.6 us
  blocking collectives  31.1 us (66%)
  Pallas kernels  7.66 us (16%)
  starting transfers between devices  4.94 us (11%)
  waiting for transfers between devices  2.93 us (6%)
    all_to_all x1, blocking collectives, per_device(): lax.all_to_all(sent, 'z', 0, 0, tiled=True, axis_index_groups=[[int(z) fo...  15.6 us
    all_to_all x1, blocking collectives, per_device(): lax.all_to_all(turn(got), ('w', 'c', 'y', 's'), 0, 0, tiled=True, axis_in...  15.5 us
    ppermute x1, starting transfers between devices, per_device(): left = lax.ppermute(own, CHAN, [(i, (i + 1) % count) for i in range(count)])  4.94 us
    pallas_call x1, Pallas kernels, denoise(): pl.pallas_call(denoise_kernel, out_shape=jax.ShapeDtypeStruct((64, 128),...  3.78 us
    ppermute x1, waiting for transfers between devices, per_device(): left = lax.ppermute(own, CHAN, [(i, (i + 1) % count) for i in range(count)])  2.93 us
    pallas_call x1, Pallas kernels, prepare(): pl.pallas_call(prepare_kernel, out_shape=(jax.ShapeDtypeStruct((LAYERS, 2...  1.58 us
    pallas_call x1, Pallas kernels, coherence(): pl.pallas_call(coherence_kernel, out_shape=jax.ShapeDtypeStruct((1, 2, 12...  1.22 us
  transfers between devices with their start and end apart: 1, of which 1 were waited for; matrix products, arithmetic and copies ran while one was open for 0% of the time, Pallas kernels for 3%

profile of v7, /device:TPU:1, one launch (start us, length us, event | category | flops | bytes accessed | tf_op | source)
XLA Modules:
  0.0 46.6 jit_solution(10806499301296638621)
XLA Ops:
  0.0 0.8 %pack.1.own_ref = bf16[2,8,768]{2,1,0:T(8,128)(2,1)S(1)} custom-call(bf16[2,8,640]{2,1,0:T(8,128)(2,1)} %raw_any.1, s32[2,8]{1,0:T(2,128)} %flags_any.1), custom_call_target="tpu_custom_call" | custom-call | tf_op jit(solution)/shard_map/pack/pallas_call | solution.py:294
  0.8 4.9 %collective-permute-start = (bf16[2,8,768]{2,1,0:T(8,128)(2,1)S(1)}, bf16[2,8,768]{2,1,0:T(8,128)(2,1)S(1)}, u32[]{:S(2)}, u32[]{:S(2)}) collective-permute-start(bf16[2,8,768]{2,1,0:T(8,128)(2,1)S(1)} %pack.1.own_ref), channel_id=1, source_target_pairs={{0,2},{2,4},{4,6},{6,8},{8,10},{10,12},{12,14},{14,16},{16,18},{18... | collective-permute-start | bytes 73736 | tf_op jit(solution)/shard_map/ppermute | solution.py:377
  5.7 1.6 %prepare.1 = (bf16[3,2,192,768]{3,2,1,0:T(8,128)(2,1)S(1)}, bf16[448,48]{1,0:T(8,128)(2,1)S(1)}, bf16[8,256]{1,0:T(8,128)(2,1)S(1)}, bf16[1024,128]{1,0:T(8,128)...) custom-call(s32[1]{0:T(128)} %bitcast.1.cut_ref, ...), custom_call_target="tpu_custom_call" | custom-call | flops 2000000 | bytes 4000000 | tf_op jit(solution)/shard_map/prepare/pallas_call | solution.py:311
  7.3 2.9 %collective-permute-done.left_ref = bf16[2,8,768]{2,1,0:T(8,128)(2,1)S(1)} collective-permute-done((bf16[2,8,768]{2,1,0:T(8,128)(2,1)S(1)}, bf16[2,8,768]{2,1,0:T(8,128)(2,1)S(1)}, u32[]{:S(2)}, u32[]{:S(2)}) %collective-permute-start) | collective-permute-done | bytes 24608 | tf_op jit(solution)/shard_map/ppermute | solution.py:377
  10.3 3.8 %denoise.1 = bf16[64,128]{1,0:T(8,128)(2,1)S(1)} custom-call(bf16[2,8,768]{2,1,0:T(8,128)(2,1)S(1)} %pack.1.own_ref, bf16[2,8,768]{2,1,0:T(8,128)(2,1)S(1)} %collective-permute-done.left_ref, bf16[640,640]{1,0:T(8,128)(2,1)S(1)} %get-tuple-element.14.order_ref, bf16[3,2,192,768]{3,2,1,0:T(8,128)(2,1)S(1)} %get-tuple-element.15.band_ref, ...), custom_call_target="tpu_custom_call" | custom-call | tf_op jit(solution)/shard_map/denoise/pallas_call | solution.py:331
  14.0 15.6 %all_to_all.22 = bf16[16,4,128]{2,1,0:T(4,128)(2,1)S(1)} all-to-all(bf16[16,4,128]{2,1,0:T(4,128)(2,1)S(1)} %bitcast.12), channel_id=1, replica_groups={{32,36,40,44,48,52,56,60,0,4,8,12,16,20,24,28},{33,37,41,45,49,53,57,61..., dimensions={0} | all-to-all | bytes 32768 | tf_op jit(solution)/shard_map/all_to_all | solution.py:383
  29.6 0.3 turn.1
  29.9 15.5 %all_to_all.23 = bf16[32,4,128]{2,1,0:T(4,128)(2,1)S(1)} all-to-all(bf16[32,4,128]{2,1,0:T(4,128)(2,1)S(1)} %bitcast.11), channel_id=1, replica_groups={{129,385,193,449,1,257,65,321,131,387,195,451,3,259,67,323,128,384,192,..., dimensions={0} | all-to-all | bytes 65536 | tf_op jit(solution)/shard_map/all_to_all | solution.py:387
  45.4 1.2 %coherence.1 = f32[1,2,128,512]{3,2,1,0:T(8,128)} custom-call(s32[1]{0:T(128)} %bitcast.half_ref, bf16[1024,128]{1,0:T(8,128)(2,1)S(1)} %get-tuple-element.20.one_hot_ref, bf16[256,256]{1,0:T(8,128)(2,1)S(1)} %get-tuple-element.21.perm_ref, bf16[128,128]{1,0:T(8,128)(2,1)S(1)} %bitcast.10), custom_call_target="tpu_custom_call" | custom-call | tf_op jit(solution)/shard_map/coherence/pallas_call | solution.py:356
Async XLA Ops:
  0.8 9.5 %collective-permute-start = (bf16[2,8,768]{2,1,0:T(8,128)(2,1)S(1)}, bf16[2,8,768]{2,1,0:T(8,128)(2,1)S(1)}, u32[]{:S(2)}, u32[]{:S(2)}) collective-permute-start(bf16[2,8,768]{2,1,0:T(8,128)(2,1)S(1)} %pack.1.own_ref), channel_id=1, source_target_pairs={{0,2},{2,4},{4,6},{6,8},{8,10},{10,12},{12,14},{14,16},{16,18},{18... | collective-permute-start | bytes 73736 | tf_op jit(solution)/shard_map/ppermute | solution.py:377

commit v8 on v7

--- a/solution.py
+++ b/solution.py
@@ -25,7 +25,7 @@
 NV = 128
 Y_ORDER = (2, 3, 0, 1)
 W_ORDER = (1, 0)
-Z_ORDER = tuple((np.arange(16) + 8) % 16)
+Z_ORDER = (8, 0, 1, 15, 2, 14, 3, 13, 4, 12, 5, 11, 6, 10, 7, 9)
 
 water_level = 0.2
 epsilon_power = 1e-06
@@ -124,7 +124,9 @@
     copies[3].wait()
     shape = (CH_ALL, NV)
     j = (sources_ref[...] + OWN // 2) % CH_ALL
-    z = ((j // 16) % 16 - Z_ORDER[0]) % 16
+    z = jnp.zeros_like(j)
+    for place, member in enumerate(Z_ORDER):
+        z = jnp.where((j // 16) % 16 == member, place, z)
     row = (j // 256) * 256 + ((j // 8) % 2) * 128 + (j % 8) * 16 + z
     one_hot_ref[...] = jnp.where(iota(shape, 0) == jnp.broadcast_to(row, shape), 1.0, 0.0).astype(BF16)
     copies[0].wait()

time: 46.9 us -> 46.9 us (level)
  no operation moved by 1% of the time
where the time goes in v8:
time: 46.9 us; the launch traced here: 46.6 us
  blocking collectives  31.1 us (66%)
  Pallas kernels  7.65 us (16%)
  starting transfers between devices  4.94 us (11%)
  waiting for transfers between devices  2.93 us (6%)
    all_to_all x1, blocking collectives, per_device(): lax.all_to_all(sent, 'z', 0, 0, tiled=True, axis_index_groups=[[int(z) fo...  15.6 us
    all_to_all x1, blocking collectives, per_device(): lax.all_to_all(turn(got), ('w', 'c', 'y', 's'), 0, 0, tiled=True, axis_in...  15.5 us
    ppermute x1, starting transfers between devices, per_device(): left = lax.ppermute(own, CHAN, [(i, (i + 1) % count) for i in range(count)])  4.94 us
    pallas_call x1, Pallas kernels, denoise(): pl.pallas_call(denoise_kernel, out_shape=jax.ShapeDtypeStruct((64, 128),...  3.78 us
    ppermute x1, waiting for transfers between devices, per_device(): left = lax.ppermute(own, CHAN, [(i, (i + 1) % count) for i in range(count)])  2.93 us
    pallas_call x1, Pallas kernels, prepare(): pl.pallas_call(prepare_kernel, out_shape=(jax.ShapeDtypeStruct((LAYERS, 2...  1.58 us
    pallas_call x1, Pallas kernels, coherence(): pl.pallas_call(coherence_kernel, out_shape=jax.ShapeDtypeStruct((1, 2, 12...  1.22 us
  transfers between devices with their start and end apart: 1, of which 1 were waited for; matrix products, arithmetic and copies ran while one was open for 0% of the time, Pallas kernels for 3%

profile of v8, /device:TPU:1, one launch (start us, length us, event | category | flops | bytes accessed | tf_op | source)
XLA Modules:
  0.0 46.6 jit_solution(10054043437444381940)
XLA Ops:
  0.0 0.8 %pack.1.own_ref = bf16[2,8,768]{2,1,0:T(8,128)(2,1)S(1)} custom-call(bf16[2,8,640]{2,1,0:T(8,128)(2,1)} %raw_any.1, s32[2,8]{1,0:T(2,128)} %flags_any.1), custom_call_target="tpu_custom_call" | custom-call | tf_op jit(solution)/shard_map/pack/pallas_call | solution.py:296
  0.8 4.9 %collective-permute-start = (bf16[2,8,768]{2,1,0:T(8,128)(2,1)S(1)}, bf16[2,8,768]{2,1,0:T(8,128)(2,1)S(1)}, u32[]{:S(2)}, u32[]{:S(2)}) collective-permute-start(bf16[2,8,768]{2,1,0:T(8,128)(2,1)S(1)} %pack.1.own_ref), channel_id=1, source_target_pairs={{0,2},{2,4},{4,6},{6,8},{8,10},{10,12},{12,14},{14,16},{16,18},{18... | collective-permute-start | bytes 73736 | tf_op jit(solution)/shard_map/ppermute | solution.py:379
  5.7 1.6 %prepare.1 = (bf16[3,2,192,768]{3,2,1,0:T(8,128)(2,1)S(1)}, bf16[448,48]{1,0:T(8,128)(2,1)S(1)}, bf16[8,256]{1,0:T(8,128)(2,1)S(1)}, bf16[1024,128]{1,0:T(8,128)...) custom-call(s32[1]{0:T(128)} %bitcast.1.cut_ref, ...), custom_call_target="tpu_custom_call" | custom-call | flops 2000000 | bytes 4000000 | tf_op jit(solution)/shard_map/prepare/pallas_call | solution.py:313
  7.3 2.9 %collective-permute-done.left_ref = bf16[2,8,768]{2,1,0:T(8,128)(2,1)S(1)} collective-permute-done((bf16[2,8,768]{2,1,0:T(8,128)(2,1)S(1)}, bf16[2,8,768]{2,1,0:T(8,128)(2,1)S(1)}, u32[]{:S(2)}, u32[]{:S(2)}) %collective-permute-start) | collective-permute-done | bytes 24608 | tf_op jit(solution)/shard_map/ppermute | solution.py:379
  10.3 3.8 %denoise.1 = bf16[64,128]{1,0:T(8,128)(2,1)S(1)} custom-call(bf16[2,8,768]{2,1,0:T(8,128)(2,1)S(1)} %pack.1.own_ref, bf16[2,8,768]{2,1,0:T(8,128)(2,1)S(1)} %collective-permute-done.left_ref, bf16[640,640]{1,0:T(8,128)(2,1)S(1)} %get-tuple-element.14.order_ref, bf16[3,2,192,768]{3,2,1,0:T(8,128)(2,1)S(1)} %get-tuple-element.15.band_ref, ...), custom_call_target="tpu_custom_call" | custom-call | tf_op jit(solution)/shard_map/denoise/pallas_call | solution.py:333
  14.0 15.6 %all_to_all.22 = bf16[16,4,128]{2,1,0:T(4,128)(2,1)S(1)} all-to-all(bf16[16,4,128]{2,1,0:T(4,128)(2,1)S(1)} %bitcast.12), channel_id=1, replica_groups={{32,0,4,60,8,56,12,52,16,48,20,44,24,40,28,36},{33,1,5,61,9,57,13,53,17..., dimensions={0} | all-to-all | bytes 32768 | tf_op jit(solution)/shard_map/all_to_all | solution.py:385
  29.6 0.3 turn.1
  29.9 15.5 %all_to_all.23 = bf16[32,4,128]{2,1,0:T(4,128)(2,1)S(1)} all-to-all(bf16[32,4,128]{2,1,0:T(4,128)(2,1)S(1)} %bitcast.11), channel_id=1, replica_groups={{129,385,193,449,1,257,65,321,131,387,195,451,3,259,67,323,128,384,192,..., dimensions={0} | all-to-all | bytes 65536 | tf_op jit(solution)/shard_map/all_to_all | solution.py:389
  45.4 1.2 %coherence.1 = f32[1,2,128,512]{3,2,1,0:T(8,128)} custom-call(s32[1]{0:T(128)} %bitcast.half_ref, bf16[1024,128]{1,0:T(8,128)(2,1)S(1)} %get-tuple-element.20.one_hot_ref, bf16[256,256]{1,0:T(8,128)(2,1)S(1)} %get-tuple-element.21.perm_ref, bf16[128,128]{1,0:T(8,128)(2,1)S(1)} %bitcast.10), custom_call_target="tpu_custom_call" | custom-call | tf_op jit(solution)/shard_map/coherence/pallas_call | solution.py:358
Async XLA Ops:
  0.8 9.5 %collective-permute-start = (bf16[2,8,768]{2,1,0:T(8,128)(2,1)S(1)}, bf16[2,8,768]{2,1,0:T(8,128)(2,1)S(1)}, u32[]{:S(2)}, u32[]{:S(2)}) collective-permute-start(bf16[2,8,768]{2,1,0:T(8,128)(2,1)S(1)} %pack.1.own_ref), channel_id=1, source_target_pairs={{0,2},{2,4},{4,6},{6,8},{8,10},{10,12},{12,14},{14,16},{16,18},{18... | collective-permute-start | bytes 73736 | tf_op jit(solution)/shard_map/ppermute | solution.py:379

commit v9 on v8

--- a/solution.py
+++ b/solution.py
@@ -23,7 +23,7 @@
 WIDE = WIN * NT
 CH_ALL = 1024
 NV = 128
-Y_ORDER = (2, 3, 0, 1)
+Y_ORDER = (2, 0, 1, 3)
 W_ORDER = (1, 0)
 Z_ORDER = (8, 0, 1, 15, 2, 14, 3, 13, 4, 12, 5, 11, 6, 10, 7, 9)
 

time: 46.9 us -> 46.9 us (level)
  no operation moved by 1% of the time
where the time goes in v9:
time: 46.9 us; the launch traced here: 46.6 us
  blocking collectives  31.1 us (66%)
  Pallas kernels  7.66 us (16%)
  starting transfers between devices  4.94 us (11%)
  waiting for transfers between devices  2.93 us (6%)
    all_to_all x1, blocking collectives, per_device(): lax.all_to_all(sent, 'z', 0, 0, tiled=True, axis_index_groups=[[int(z) fo...  15.6 us
    all_to_all x1, blocking collectives, per_device(): lax.all_to_all(turn(got), ('w', 'c', 'y', 's'), 0, 0, tiled=True, axis_in...  15.5 us
    ppermute x1, starting transfers between devices, per_device(): left = lax.ppermute(own, CHAN, [(i, (i + 1) % count) for i in range(count)])  4.94 us
    pallas_call x1, Pallas kernels, denoise(): pl.pallas_call(denoise_kernel, out_shape=jax.ShapeDtypeStruct((64, 128),...  3.78 us
    ppermute x1, waiting for transfers between devices, per_device(): left = lax.ppermute(own, CHAN, [(i, (i + 1) % count) for i in range(count)])  2.93 us
    pallas_call x1, Pallas kernels, prepare(): pl.pallas_call(prepare_kernel, out_shape=(jax.ShapeDtypeStruct((LAYERS, 2...  1.58 us
    pallas_call x1, Pallas kernels, coherence(): pl.pallas_call(coherence_kernel, out_shape=jax.ShapeDtypeStruct((1, 2, 12...  1.22 us
  transfers between devices with their start and end apart: 1, of which 1 were waited for; matrix products, arithmetic and copies ran while one was open for 0% of the time, Pallas kernels for 3%

profile of v9, /device:TPU:1, one launch (start us, length us, event | category | flops | bytes accessed | tf_op | source)
XLA Modules:
  0.0 46.6 jit_solution(14244528619026813917)
XLA Ops:
  0.0 0.8 %pack.1.own_ref = bf16[2,8,768]{2,1,0:T(8,128)(2,1)S(1)} custom-call(bf16[2,8,640]{2,1,0:T(8,128)(2,1)} %raw_any.1, s32[2,8]{1,0:T(2,128)} %flags_any.1), custom_call_target="tpu_custom_call" | custom-call | tf_op jit(solution)/shard_map/pack/pallas_call | solution.py:296
  0.8 4.9 %collective-permute-start = (bf16[2,8,768]{2,1,0:T(8,128)(2,1)S(1)}, bf16[2,8,768]{2,1,0:T(8,128)(2,1)S(1)}, u32[]{:S(2)}, u32[]{:S(2)}) collective-permute-start(bf16[2,8,768]{2,1,0:T(8,128)(2,1)S(1)} %pack.1.own_ref), channel_id=1, source_target_pairs={{0,2},{2,4},{4,6},{6,8},{8,10},{10,12},{12,14},{14,16},{16,18},{18... | collective-permute-start | bytes 73736 | tf_op jit(solution)/shard_map/ppermute | solution.py:379
  5.7 1.6 %prepare.1 = (bf16[3,2,192,768]{3,2,1,0:T(8,128)(2,1)S(1)}, bf16[448,48]{1,0:T(8,128)(2,1)S(1)}, bf16[8,256]{1,0:T(8,128)(2,1)S(1)}, bf16[1024,128]{1,0:T(8,128)...) custom-call(s32[1]{0:T(128)} %bitcast.1.cut_ref, ...), custom_call_target="tpu_custom_call" | custom-call | flops 2000000 | bytes 4000000 | tf_op jit(solution)/shard_map/prepare/pallas_call | solution.py:313
  7.3 2.9 %collective-permute-done.left_ref = bf16[2,8,768]{2,1,0:T(8,128)(2,1)S(1)} collective-permute-done((bf16[2,8,768]{2,1,0:T(8,128)(2,1)S(1)}, bf16[2,8,768]{2,1,0:T(8,128)(2,1)S(1)}, u32[]{:S(2)}, u32[]{:S(2)}) %collective-permute-start) | collective-permute-done | bytes 24608 | tf_op jit(solution)/shard_map/ppermute | solution.py:379
  10.3 3.8 %denoise.1 = bf16[64,128]{1,0:T(8,128)(2,1)S(1)} custom-call(bf16[2,8,768]{2,1,0:T(8,128)(2,1)S(1)} %pack.1.own_ref, bf16[2,8,768]{2,1,0:T(8,128)(2,1)S(1)} %collective-permute-done.left_ref, bf16[640,640]{1,0:T(8,128)(2,1)S(1)} %get-tuple-element.14.order_ref, bf16[3,2,192,768]{3,2,1,0:T(8,128)(2,1)S(1)} %get-tuple-element.15.band_ref, ...), custom_call_target="tpu_custom_call" | custom-call | tf_op jit(solution)/shard_map/denoise/pallas_call | solution.py:333
  14.0 15.6 %all_to_all.22 = bf16[16,4,128]{2,1,0:T(4,128)(2,1)S(1)} all-to-all(bf16[16,4,128]{2,1,0:T(4,128)(2,1)S(1)} %bitcast.12), channel_id=1, replica_groups={{32,0,4,60,8,56,12,52,16,48,20,44,24,40,28,36},{33,1,5,61,9,57,13,53,17..., dimensions={0} | all-to-all | bytes 32768 | tf_op jit(solution)/shard_map/all_to_all | solution.py:385
  29.6 0.3 turn.1
  29.9 15.5 %all_to_all.23 = bf16[32,4,128]{2,1,0:T(4,128)(2,1)S(1)} all-to-all(bf16[32,4,128]{2,1,0:T(4,128)(2,1)S(1)} %bitcast.11), channel_id=1, replica_groups={{129,385,1,257,65,321,193,449,131,387,3,259,67,323,195,451,128,384,0,25..., dimensions={0} | all-to-all | bytes 65536 | tf_op jit(solution)/shard_map/all_to_all | solution.py:389
  45.4 1.2 %coherence.1 = f32[1,2,128,512]{3,2,1,0:T(8,128)} custom-call(s32[1]{0:T(128)} %bitcast.half_ref, bf16[1024,128]{1,0:T(8,128)(2,1)S(1)} %get-tuple-element.20.one_hot_ref, bf16[256,256]{1,0:T(8,128)(2,1)S(1)} %get-tuple-element.21.perm_ref, bf16[128,128]{1,0:T(8,128)(2,1)S(1)} %bitcast.10), custom_call_target="tpu_custom_call" | custom-call | tf_op jit(solution)/shard_map/coherence/pallas_call | solution.py:358
Async XLA Ops:
  0.8 9.5 %collective-permute-start = (bf16[2,8,768]{2,1,0:T(8,128)(2,1)S(1)}, bf16[2,8,768]{2,1,0:T(8,128)(2,1)S(1)}, u32[]{:S(2)}, u32[]{:S(2)}) collective-permute-start(bf16[2,8,768]{2,1,0:T(8,128)(2,1)S(1)} %pack.1.own_ref), channel_id=1, source_target_pairs={{0,2},{2,4},{4,6},{6,8},{8,10},{10,12},{12,14},{14,16},{16,18},{18... | collective-permute-start | bytes 73736 | tf_op jit(solution)/shard_map/ppermute | solution.py:379

commit v10 on v8

--- a/solution.py
+++ b/solution.py
@@ -279,9 +279,16 @@
     left = chosen_t.astype(BF16)
     copies = []
     for part, right in enumerate((receivers, turned)):
-        out_ref[part] = jnp.dot(left, right.astype(BF16), preferred_element_type=F32) * scale
-        copies.append(pltpu.make_async_copy(out_ref.at[part], out_any.at[0, part], sems.at[part]))
-        copies[-1].start()
+        right = right.astype(BF16)
+        for i in range(2):
+            rows = slice(i * 64, (i + 1) * 64)
+            out_ref[part, rows] = jnp.dot(left[rows], right, preferred_element_type=F32) * scale[rows]
+            copies.append(
+                pltpu.make_async_copy(
+                    out_ref.at[part, rows], out_any.at[0, part, rows], sems.at[2 * part + i]
+                )
+            )
+            copies[-1].start()
     for copy in copies:
         copy.wait()
 
@@ -363,7 +370,7 @@
         scratch_shapes=[
             pltpu.VMEM((16, CH_ALL), F32),
             pltpu.VMEM((2, 128, 512), F32),
-            pltpu.SemaphoreType.DMA((2,)),
+            pltpu.SemaphoreType.DMA((4,)),
         ],
         compiler_params=PARAMS,
         name="coherence",

time: 46.9 us -> 46.9 us (level)
  no operation moved by 1% of the time
where the time goes in v10:
time: 46.9 us; the launch traced here: 46.6 us
  blocking collectives  31.1 us (66%)
  Pallas kernels  7.65 us (16%)
  starting transfers between devices  4.94 us (11%)
  waiting for transfers between devices  2.93 us (6%)
    all_to_all x1, blocking collectives, per_device(): lax.all_to_all(sent, 'z', 0, 0, tiled=True, axis_index_groups=[[int(z) fo...  15.6 us
    all_to_all x1, blocking collectives, per_device(): lax.all_to_all(turn(got), ('w', 'c', 'y', 's'), 0, 0, tiled=True, axis_in...  15.5 us
    ppermute x1, starting transfers between devices, per_device(): left = lax.ppermute(own, CHAN, [(i, (i + 1) % count) for i in range(count)])  4.94 us
    pallas_call x1, Pallas kernels, denoise(): pl.pallas_call(denoise_kernel, out_shape=jax.ShapeDtypeStruct((64, 128),...  3.78 us
    ppermute x1, waiting for transfers between devices, per_device(): left = lax.ppermute(own, CHAN, [(i, (i + 1) % count) for i in range(count)])  2.93 us
    pallas_call x1, Pallas kernels, prepare(): pl.pallas_call(prepare_kernel, out_shape=(jax.ShapeDtypeStruct((LAYERS, 2...  1.58 us
    pallas_call x1, Pallas kernels, coherence(): pl.pallas_call(coherence_kernel, out_shape=jax.ShapeDtypeStruct((1, 2, 12...  1.21 us
  transfers between devices with their start and end apart: 1, of which 1 were waited for; matrix products, arithmetic and copies ran while one was open for 0% of the time, Pallas kernels for 3%

profile of v10, /device:TPU:1, one launch (start us, length us, event | category | flops | bytes accessed | tf_op | source)
XLA Modules:
  0.0 46.6 jit_solution(5243991235177118971)
XLA Ops:
  0.0 0.8 %pack.1.own_ref = bf16[2,8,768]{2,1,0:T(8,128)(2,1)S(1)} custom-call(bf16[2,8,640]{2,1,0:T(8,128)(2,1)} %raw_any.1, s32[2,8]{1,0:T(2,128)} %flags_any.1), custom_call_target="tpu_custom_call" | custom-call | tf_op jit(solution)/shard_map/pack/pallas_call | solution.py:303
  0.8 4.9 %collective-permute-start = (bf16[2,8,768]{2,1,0:T(8,128)(2,1)S(1)}, bf16[2,8,768]{2,1,0:T(8,128)(2,1)S(1)}, u32[]{:S(2)}, u32[]{:S(2)}) collective-permute-start(bf16[2,8,768]{2,1,0:T(8,128)(2,1)S(1)} %pack.1.own_ref), channel_id=1, source_target_pairs={{0,2},{2,4},{4,6},{6,8},{8,10},{10,12},{12,14},{14,16},{16,18},{18... | collective-permute-start | bytes 73736 | tf_op jit(solution)/shard_map/ppermute | solution.py:386
  5.7 1.6 %prepare.1 = (bf16[3,2,192,768]{3,2,1,0:T(8,128)(2,1)S(1)}, bf16[448,48]{1,0:T(8,128)(2,1)S(1)}, bf16[8,256]{1,0:T(8,128)(2,1)S(1)}, bf16[1024,128]{1,0:T(8,128)...) custom-call(s32[1]{0:T(128)} %bitcast.1.cut_ref, ...), custom_call_target="tpu_custom_call" | custom-call | flops 2000000 | bytes 4000000 | tf_op jit(solution)/shard_map/prepare/pallas_call | solution.py:320
  7.3 2.9 %collective-permute-done.left_ref = bf16[2,8,768]{2,1,0:T(8,128)(2,1)S(1)} collective-permute-done((bf16[2,8,768]{2,1,0:T(8,128)(2,1)S(1)}, bf16[2,8,768]{2,1,0:T(8,128)(2,1)S(1)}, u32[]{:S(2)}, u32[]{:S(2)}) %collective-permute-start) | collective-permute-done | bytes 24608 | tf_op jit(solution)/shard_map/ppermute | solution.py:386
  10.3 3.8 %denoise.1 = bf16[64,128]{1,0:T(8,128)(2,1)S(1)} custom-call(bf16[2,8,768]{2,1,0:T(8,128)(2,1)S(1)} %pack.1.own_ref, bf16[2,8,768]{2,1,0:T(8,128)(2,1)S(1)} %collective-permute-done.left_ref, bf16[640,640]{1,0:T(8,128)(2,1)S(1)} %get-tuple-element.14.order_ref, bf16[3,2,192,768]{3,2,1,0:T(8,128)(2,1)S(1)} %get-tuple-element.15.band_ref, ...), custom_call_target="tpu_custom_call" | custom-call | tf_op jit(solution)/shard_map/denoise/pallas_call | solution.py:340
  14.0 15.6 %all_to_all.22 = bf16[16,4,128]{2,1,0:T(4,128)(2,1)S(1)} all-to-all(bf16[16,4,128]{2,1,0:T(4,128)(2,1)S(1)} %bitcast.12), channel_id=1, replica_groups={{32,0,4,60,8,56,12,52,16,48,20,44,24,40,28,36},{33,1,5,61,9,57,13,53,17..., dimensions={0} | all-to-all | bytes 32768 | tf_op jit(solution)/shard_map/all_to_all | solution.py:392
  29.6 0.3 turn.1
  29.9 15.5 %all_to_all.23 = bf16[32,4,128]{2,1,0:T(4,128)(2,1)S(1)} all-to-all(bf16[32,4,128]{2,1,0:T(4,128)(2,1)S(1)} %bitcast.11), channel_id=1, replica_groups={{129,385,193,449,1,257,65,321,131,387,195,451,3,259,67,323,128,384,192,..., dimensions={0} | all-to-all | bytes 65536 | tf_op jit(solution)/shard_map/all_to_all | solution.py:396
  45.4 1.2 %coherence.1 = f32[1,2,128,512]{3,2,1,0:T(8,128)} custom-call(s32[1]{0:T(128)} %bitcast.half_ref, bf16[1024,128]{1,0:T(8,128)(2,1)S(1)} %get-tuple-element.20.one_hot_ref, bf16[256,256]{1,0:T(8,128)(2,1)S(1)} %get-tuple-element.21.perm_ref, bf16[128,128]{1,0:T(8,128)(2,1)S(1)} %bitcast.10), custom_call_target="tpu_custom_call" | custom-call | tf_op jit(solution)/shard_map/coherence/pallas_call | solution.py:365
Async XLA Ops:
  0.8 9.5 %collective-permute-start = (bf16[2,8,768]{2,1,0:T(8,128)(2,1)S(1)}, bf16[2,8,768]{2,1,0:T(8,128)(2,1)S(1)}, u32[]{:S(2)}, u32[]{:S(2)}) collective-permute-start(bf16[2,8,768]{2,1,0:T(8,128)(2,1)S(1)} %pack.1.own_ref), channel_id=1, source_target_pairs={{0,2},{2,4},{4,6},{6,8},{8,10},{10,12},{12,14},{14,16},{16,18},{18... | collective-permute-start | bytes 73736 | tf_op jit(solution)/shard_map/ppermute | solution.py:386
